TPU v7x, 256 devices: a whole 4x4x8 slice. The times are simulated.
256 devices in a mesh: row: 4 (over y_hi, core), col: 16 (over y_lo, z), tm: 4 (over x).
Axes of the slice: x: 4, y: 4 (y_hi: 2, y_lo: 2; y = y_hi * 2 + y_lo), z: 8, core: 2. Of those that a mesh axis runs over, the one named last changes fastest.
Arguments:
- traces: bfloat16 [2048, 128, 512], P(('row', 'col'), 'tm'), may hold values from -6 to 6
- live_flags: int32 [2048], P(('row', 'col')), may hold values 0 or 1
Outputs:
- stacks: bfloat16 [2048, 256, 256], P(('row', 'col', 'tm'))
Inputs may be any that keep to these rules, and one draw needn't show every extreme that they name: `live_flags`: dead channels are 0, working ones 1.
All inputs are finite; a program needn't handle non-finite values. No bound on the sum of `live_flags` on one device may be relied on, other than what follows from the above.
Results may differ from a plain program's by a relative error of at most 0.006.
Values may be sent and summed in bfloat16 or wider, within the bound.
No kernel may reach another device: no remote copies, remote signals or barrier semaphores. Data moves between devices by JAX's collectives and lax.ppermute only.
A program may use at most 128 MiB of HBM per device.

v0:
```python
import jax
import jax.numpy as jnp
from jax import lax
from jax.sharding import PartitionSpec as P

NFFT = 512
OFFS = 256
LAGS = 256
SMOOTH = 32


def from_behind(value, axis, steps):
    count = lax.axis_size(axis)
    initial, last = (max(0, -steps), min(count, count - steps))
    return lax.ppermute(value, axis, [(source, source + steps) for source in range(initial, last)])


def dft_table(fft_length):
    sample_index = jnp.arange(fft_length, dtype=jnp.float32)[:, None]
    bin_values = jnp.arange(fft_length // 2, dtype=jnp.float32)[None, :]
    hann_taper = 0.5 - 0.5 * jnp.cos(2.0 * jnp.pi * sample_index / fft_length)
    phase_angle = 2.0 * jnp.pi * jnp.mod(sample_index * bin_values, fft_length) / fft_length
    columns = jnp.concatenate(
        [hann_taper * jnp.cos(phase_angle), -hann_taper * jnp.sin(phase_angle)], axis=1
    )
    return columns.astype(jnp.bfloat16)


def whiten_tile(traces_tile, flags_tile, smooth_half):
    channels_here, minutes_here, fft_length = traces_tile.shape
    half_length = fft_length // 2
    spectra = jnp.dot(
        traces_tile.reshape(channels_here * minutes_here, fft_length),
        dft_table(fft_length),
        preferred_element_type=jnp.float32,
    )
    spec_real = spectra[:, :half_length]
    spec_imag = spectra[:, half_length:]
    power_sum = spec_real * spec_real + spec_imag * spec_imag
    bin_index = jnp.arange(half_length)
    band_matrix = (jnp.abs(bin_index[:, None] - bin_index[None, :]) <= smooth_half).astype(
        jnp.float32
    )
    bin_count = jnp.sum(band_matrix, axis=0)
    smoothed = jnp.dot(power_sum, band_matrix, precision=lax.Precision.HIGHEST) / bin_count
    live_rows = jnp.repeat(flags_tile.astype(jnp.float32), minutes_here)[:, None]
    inverse_amp = live_rows * lax.rsqrt(smoothed + 1e-06)
    whitened = jnp.concatenate([spec_real * inverse_amp, spec_imag * inverse_amp], axis=1)
    return whitened.astype(jnp.bfloat16).reshape(channels_here, minutes_here, fft_length)


def lag_tables(fft_length, lag_count, bin_width):
    bin_values = jnp.arange(bin_width).astype(jnp.float32)[:, None]
    lag_index = (jnp.arange(lag_count) - lag_count // 2).astype(jnp.float32)[None, :]
    weight = jnp.where(bin_values == 0, 1.0, 2.0) / fft_length
    phase_angle = 2.0 * jnp.pi * jnp.mod(bin_values * lag_index, fft_length) / fft_length
    return (weight * jnp.cos(phase_angle), -weight * jnp.sin(phase_angle))


def skew_cut_last(cross_block, offs):
    row_count, col_width, bin_width = cross_block.shape
    flattened = cross_block.reshape(row_count * col_width, bin_width)
    flattened = jnp.pad(flattened, ((0, row_count), (0, 0)))
    skew_grid = flattened.reshape(row_count, col_width + 1, bin_width)
    return skew_grid[:, 1 : 1 + offs, :]


def cross_window(own_rows, window, offs):
    row_count, minutes_here, width = own_rows.shape
    bin_width = width // 2
    rows_parts = own_rows.reshape(row_count, minutes_here, 2, bin_width)
    turned = jnp.stack([rows_parts[:, :, 1], -rows_parts[:, :, 0]], axis=2)
    cols_parts = window.reshape(window.shape[0], minutes_here, 2, bin_width)
    cross_real = jnp.einsum(
        "cmpk,jmpk->cjk", rows_parts, cols_parts, preferred_element_type=jnp.float32
    )
    cross_imag = jnp.einsum(
        "cmpk,jmpk->cjk", turned, cols_parts, preferred_element_type=jnp.float32
    )
    return (skew_cut_last(cross_real, offs), skew_cut_last(cross_imag, offs))


def lag_transform(cross_real, cross_imag, half_length):
    cos_table, sin_table = lag_tables(NFFT, LAGS, half_length)
    both_tables = jnp.concatenate([cos_table, sin_table], axis=0)
    both_parts = jnp.concatenate([cross_real, cross_imag], axis=2)
    return jnp.einsum("cok,kt->cot", both_parts, both_tables, precision=lax.Precision.HIGHEST)


def body(traces, live_flags):
    own_tile = whiten_tile(traces, live_flags, SMOOTH)
    channels_here, minutes_here, fft_length = own_tile.shape
    half_length = fft_length // 2
    reach_tiles = OFFS // channels_here
    tile_list = [own_tile] + [
        from_behind(own_tile, ("row", "col"), -neighbour) for neighbour in range(1, reach_tiles + 1)
    ]
    band_window = jnp.concatenate(tile_list, axis=0)
    cross_real, cross_imag = cross_window(own_tile, band_window, OFFS)
    stacked = lax.psum_scatter(
        lag_transform(cross_real, cross_imag, half_length), "tm", scatter_dimension=0, tiled=True
    )
    return stacked.astype(jnp.bfloat16)


def solution(mesh):
    return jax.shard_map(
        body,
        mesh=mesh,
        in_specs=(P(("row", "col"), "tm", None), P(("row", "col"))),
        out_specs=P(("row", "col", "tm"), None, None),
        check_vma=False,
    )
```

profile of v0, /device:TPU:1, one launch (start us, length us, event | category | flops | bytes accessed | tf_op | source)
XLA Modules:
  0.0 549.9 jit_solution(13492681819078665016)
XLA Ops:
  6.6 0.1 convert_reduce_fusion
  6.7 0.8 convert_element_type.48
  7.5 0.1 broadcast_in_dim.8
  7.5 0.1 mul.122
  7.6 2.4 multiply_convert_fusion.2
  10.1 0.8 convolution_bitcast_fusion.2
  10.8 1.1 multiply_convert_fusion.1
  11.9 0.2 copy.56
  12.1 0.6 copy-done.4
  12.7 0.2 copy.57
  12.9 1.1 pad_maximum_fusion.2
  14.0 9.9 %collective-permute-start = (bf16[32,32,512]{2,1,0:T(8,128)(2,1)}, bf16[32,32,512]{2,1,0:T(8,128)(2,1)}, u32[]{:S(2)}, u32[]{:S(2)}) collective-permute-start(bf16[32,32,512]{2,1,0:T(8,128)(2,1)} %pad_maximum_fusion.2), channel_id=1, source_target_pairs={{4,0},{8,4},{12,8},{16,12},{20,16},{24,20},{28,24},{32,28},{36,32}... | collective-permute-start | bytes 3145736 | tf_op jit(solution)/shard_map/ppermute | solution.py:15
  23.8 3.4 collective-permute-start.1
  27.2 2.4 collective-permute-start.2
  29.6 6.8 %collective-permute-start.3 = (bf16[32,32,512]{2,1,0:T(8,128)(2,1)}, bf16[32,32,512]{2,1,0:T(8,128)(2,1)}, u32[]{:S(2)}, u32[]{:S(2)}) collective-permute-start(bf16[32,32,512]{2,1,0:T(8,128)(2,1)} %pad_maximum_fusion.2), channel_id=1, source_target_pairs={{16,0},{20,4},{24,8},{28,12},{32,16},{36,20},{40,24},{44,28},{48,3... | collective-permute-start | bytes 3145736 | tf_op jit(solution)/shard_map/ppermute | solution.py:15
  36.4 1.9 collective-permute-start.4
  38.4 3.2 copy.58
  41.6 3.9 copy.59
  45.5 1.3 pad_maximum_fusion.1
  46.8 1.3 copy.70
  48.1 1.3 convert_element_type.50
  49.5 5.9 %copy.71 = bf16[32,32,2,256]{1,0,2,3:T(8,128)(2,1)} copy(bf16[32,32,2,256]{3,2,1,0:T(2,128)(2,1)S(1)} %convert_element_type.50) | data formatting | bytes 2097152 | tf_op jit(solution)/shard_map/convert_element_type | solution.py:49
  55.4 0.0 collective-permute-done
  55.4 1.9 collective-permute-start.5
  57.3 28.8 %collective-permute-done.1 = bf16[32,32,512]{2,1,0:T(8,128)(2,1)} collective-permute-done((bf16[32,32,512]{2,1,0:T(8,128)(2,1)}, bf16[32,32,512]{2,1,0:T(8,128)(2,1)}, u32[]{:S(2)}, u32[]{:S(2)}) %collective-permute-start.1) | collective-permute-done | bytes 1048608 | tf_op jit(solution)/shard_map/ppermute | solution.py:15
  86.0 1.9 collective-permute-start.6
  88.0 69.1 %collective-permute-done.2 = bf16[32,32,512]{2,1,0:T(8,128)(2,1)} collective-permute-done((bf16[32,32,512]{2,1,0:T(8,128)(2,1)}, bf16[32,32,512]{2,1,0:T(8,128)(2,1)}, u32[]{:S(2)}, u32[]{:S(2)}) %collective-permute-start.2) | collective-permute-done | bytes 1048608 | tf_op jit(solution)/shard_map/ppermute | solution.py:15
  157.1 87.5 %collective-permute-start.7 = (bf16[32,32,512]{2,1,0:T(8,128)(2,1)}, bf16[32,32,512]{2,1,0:T(8,128)(2,1)}, u32[]{:S(2)}, u32[]{:S(2)}) collective-permute-start(bf16[32,32,512]{2,1,0:T(8,128)(2,1)} %pad_maximum_fusion.2), channel_id=1, source_target_pairs={{32,0},{36,4},{40,8},{44,12},{48,16},{52,20},{56,24},{60,28},{64,3... | collective-permute-start | bytes 3145736 | tf_op jit(solution)/shard_map/ppermute | solution.py:15
  244.6 4.5 pad_maximum_fusion
  249.1 2.0 cosine_multiply_fusion
  251.0 1.7 fusion.36
  252.8 1.3 concatenate.57
  254.1 6.0 %copy.62 = bf16[32,32,2,256]{0,1,2,3:T(8,128)(2,1)} copy(bf16[32,32,2,256]{3,2,1,0:T(2,128)(2,1)S(1)} %concatenate.57) | data formatting | bytes 2097152 | tf_op jit(solution)/shard_map/concatenate | solution.py:98
  260.1 1.3 concatenate.58
  261.5 6.0 %copy.63 = bf16[32,32,2,256]{0,1,2,3:T(8,128)(2,1)} copy(bf16[32,32,2,256]{3,2,1,0:T(2,128)(2,1)S(1)} %concatenate.58) | data formatting | bytes 2097152 | tf_op jit(solution)/shard_map/concatenate | solution.py:98
  267.5 1.3 concatenate.59
  268.9 6.0 %copy.64 = bf16[32,32,2,256]{0,1,2,3:T(8,128)(2,1)} copy(bf16[32,32,2,256]{3,2,1,0:T(2,128)(2,1)S(1)} %concatenate.59) | data formatting | bytes 2097152 | tf_op jit(solution)/shard_map/concatenate | solution.py:98
  274.8 0.0 collective-permute-done.3
  274.8 1.3 concatenate.60
  276.2 6.0 %copy.65 = bf16[32,32,2,256]{0,1,2,3:T(8,128)(2,1)} copy(bf16[32,32,2,256]{3,2,1,0:T(2,128)(2,1)S(1)} %concatenate.60) | data formatting | bytes 2097152 | tf_op jit(solution)/shard_map/concatenate | solution.py:98
  282.1 0.0 collective-permute-done.4
  282.1 1.3 concatenate.61
  283.5 6.0 %copy.66 = bf16[32,32,2,256]{0,1,2,3:T(8,128)(2,1)} copy(bf16[32,32,2,256]{3,2,1,0:T(2,128)(2,1)S(1)} %concatenate.61) | data formatting | bytes 2097152 | tf_op jit(solution)/shard_map/concatenate | solution.py:98
  289.5 1.3 concatenate.62
  290.8 6.0 %copy.67 = bf16[32,32,2,256]{0,1,2,3:T(8,128)(2,1)} copy(bf16[32,32,2,256]{3,2,1,0:T(2,128)(2,1)S(1)} %concatenate.62) | data formatting | bytes 2097152 | tf_op jit(solution)/shard_map/concatenate | solution.py:98
  296.8 1.3 concatenate.63
  298.1 6.0 %copy.68 = bf16[32,32,2,256]{0,1,2,3:T(8,128)(2,1)} copy(bf16[32,32,2,256]{3,2,1,0:T(2,128)(2,1)S(1)} %concatenate.63) | data formatting | bytes 2097152 | tf_op jit(solution)/shard_map/concatenate | solution.py:98
  304.1 1.3 concatenate.64
  305.5 6.0 %copy.69 = bf16[32,32,2,256]{0,1,2,3:T(8,128)(2,1)} copy(bf16[32,32,2,256]{3,2,1,0:T(2,128)(2,1)S(1)} %concatenate.64) | data formatting | bytes 2097152 | tf_op jit(solution)/shard_map/concatenate | solution.py:98
  311.4 38.0 %concatenate.65 = bf16[288,32,2,256]{0,1,2,3:T(8,128)(2,1)} concatenate(bf16[32,32,2,256]{0,1,2,3:T(8,128)(2,1)} %pad_maximum_fusion, bf16[32,32,2,256]{0,1,2,3:T(8,128)(2,1)} %copy.62, bf16[32,32,2,256]{0,1,2,3:T(8,128)(2,1)} %copy.63, bf16[32,32,2,256]{0,1,2,3:T(8,128)(2,1)} %copy.64, bf16[32,32,2,256]{0,1,2,3:T(8,128)(2,1)} %copy.65, bf16[32,32,2,256]{0,1,2,3:T(8,128)(2,1)} %copy.66, ...), dimensions={0} | concatenate | bytes 18874368 | tf_op jit(solution)/shard_map/concatenate | solution.py:98
  349.4 12.7 %convolution_bitcast_fusion.1 = f32[32,288,256]{1,0,2:T(8,128)} fusion(bf16[32,32,2,256]{1,0,2,3:T(8,128)(2,1)} %copy.71, bf16[288,32,2,256]{0,1,2,3:T(8,128)(2,1)} %concatenate.65), kind=kOutput, calls=%fused_computation.5 | convolution fusion | flops 301989888 | bytes 19922944 | tf_op jit(solution)/shard_map/cmpk,jmpk->cjk/dot_general | solution.py:74
  362.1 11.7 %copy.72 = f32[32,288,256]{2,1,0:T(8,128)} copy(f32[32,288,256]{1,0,2:T(8,128)} %convolution_bitcast_fusion.1) | data formatting | bytes 18874368 | tf_op jit(solution)/shard_map/cmpk,jmpk->cjk/transpose | solution.py:74
  373.8 6.5 %pad.7 = f32[9248,256]{1,0:T(8,128)} pad(f32[9216,256]{1,0:T(8,128)} %bitcast.28, f32[]{:T(128)} %constant.21.clone.1), padding=0_32x0_0 | pad | bytes 18907140 | tf_op jit(solution)/shard_map/jit(_pad)/pad | solution.py:63
  380.3 8.0 %reshape.78 = f32[32,289,256]{2,1,0:T(8,128)} reshape(f32[9248,256]{1,0:T(8,128)} %pad.7) | data formatting | bytes 18939904 | tf_op jit(solution)/shard_map/reshape | solution.py:64
  388.3 8.0 %slice.26 = f32[32,256,256]{2,1,0:T(8,128)} slice(f32[32,289,256]{2,1,0:T(8,128)} %reshape.78), slice={[0:32], [1:257], [0:256]} | slice | bytes 16777216 | tf_op jit(solution)/shard_map/slice | solution.py:65
  396.3 11.5 %convolution_bitcast_fusion = f32[32,288,256]{1,0,2:T(8,128)} fusion(bf16[288,32,2,256]{0,1,2,3:T(8,128)(2,1)} %concatenate.65, bf16[32,32,1,256]{1,0,2,3:T(8,128)(2,1)S(1)} %copy-done.3, bf16[32,32,1,256]{1,0,2,3:T(8,128)(2,1)S(1)} %get-tuple-element.5), kind=kOutput, calls=%fused_computation.4 | convolution fusion | flops 304087040 | bytes 19922944 | tf_op jit(solution)/shard_map/cmpk,jmpk->cjk/dot_general | solution.py:77
  407.8 11.7 %copy.75 = f32[32,288,256]{2,1,0:T(8,128)} copy(f32[32,288,256]{1,0,2:T(8,128)} %convolution_bitcast_fusion) | data formatting | bytes 18874368 | tf_op jit(solution)/shard_map/cmpk,jmpk->cjk/transpose | solution.py:77
  419.5 6.4 %pad.8 = f32[9248,256]{1,0:T(8,128)} pad(f32[9216,256]{1,0:T(8,128)} %bitcast.27, f32[]{:T(128)} %constant.21.clone.1), padding=0_32x0_0 | pad | bytes 18907140 | tf_op jit(solution)/shard_map/jit(_pad)/pad | solution.py:63
  425.9 8.0 %reshape.80 = f32[32,289,256]{2,1,0:T(8,128)} reshape(f32[9248,256]{1,0:T(8,128)} %pad.8) | data formatting | bytes 18939904 | tf_op jit(solution)/shard_map/reshape | solution.py:64
  433.9 4.6 slice.29
  438.5 17.9 %fusion = f32[32,256,256]{2,1,0:T(8,128)} fusion(f32[32,256,256]{2,1,0:T(8,128)S(1)} %slice.29, f32[32,256,256]{2,1,0:T(8,128)} %slice.26, f32[256,256]{1,0:T(8,128)S(1)} %copy-done.6, f32[256,256]{1,0:T(8,128)S(1)} %get-tuple-element.9), kind=kOutput, calls=%fused_computation | convolution fusion | flops 12889227264 | bytes 25690112 | tf_op jit(solution)/shard_map/cok,kt->cot/dot_general | solution.py:87
  456.4 0.0 reduce-scatter.2.cloned.1.call-update
  456.5 83.9 %reduce-scatter.2.cloned.1.call-done = f32[8,256,256]{2,1,0:T(8,128)} async-done(((f32[32,256,256]{2,1,0:T(8,128)}), f32[8,256,256]{2,1,0:T(8,128)}) %reduce-scatter.2.cloned.1.call-update) | async-done | bytes 2097168 | tf_op jit(solution)/shard_map/reduce_scatter | solution.py:100
  540.4 2.7 convert_element_type.53
  (21 shorter events, 0.1 us)
Async XLA Ops:
  6.5 3.5 copy-start
  6.5 533.8 %reduce-scatter.2.cloned.1.call-start = ((), (), s32[]{:S(2)}) async-start(), calls=%async_computation.1 | async-start | bytes 10485760 | tf_op jit(solution)/shard_map/reduce_scatter | solution.py:100
  11.9 0.8 copy-start.4
  11.9 26.4 %copy-start.5 = (bf16[1024,256]{0,1:T(8,128)(2,1)}, bf16[1024,256]{0,1:T(8,128)(2,1)S(1)}, u32[]{:S(2)}) copy-start(bf16[1024,256]{0,1:T(8,128)(2,1)S(1)} %get-tuple-element.8) | copy-start | bytes 1572868
  14.0 41.4 %collective-permute-start = (bf16[32,32,512]{2,1,0:T(8,128)(2,1)}, bf16[32,32,512]{2,1,0:T(8,128)(2,1)}, u32[]{:S(2)}, u32[]{:S(2)}) collective-permute-start(bf16[32,32,512]{2,1,0:T(8,128)(2,1)} %pad_maximum_fusion.2), channel_id=1, source_target_pairs={{4,0},{8,4},{12,8},{16,12},{20,16},{24,20},{28,24},{32,28},{36,32}... | collective-permute-start | bytes 3145736 | tf_op jit(solution)/shard_map/ppermute | solution.py:15
  23.8 62.2 %collective-permute-start.1 = (bf16[32,32,512]{2,1,0:T(8,128)(2,1)}, bf16[32,32,512]{2,1,0:T(8,128)(2,1)}, u32[]{:S(2)}, u32[]{:S(2)}) collective-permute-start(bf16[32,32,512]{2,1,0:T(8,128)(2,1)} %pad_maximum_fusion.2), channel_id=1, source_target_pairs={{8,0},{12,4},{16,8},{20,12},{24,16},{28,20},{32,24},{36,28},{40,32... | collective-permute-start | bytes 3145736 | tf_op jit(solution)/shard_map/ppermute | solution.py:15
  27.2 129.9 %collective-permute-start.2 = (bf16[32,32,512]{2,1,0:T(8,128)(2,1)}, bf16[32,32,512]{2,1,0:T(8,128)(2,1)}, u32[]{:S(2)}, u32[]{:S(2)}) collective-permute-start(bf16[32,32,512]{2,1,0:T(8,128)(2,1)} %pad_maximum_fusion.2), channel_id=1, source_target_pairs={{12,0},{16,4},{20,8},{24,12},{28,16},{32,20},{36,24},{40,28},{44,3... | collective-permute-start | bytes 3145736 | tf_op jit(solution)/shard_map/ppermute | solution.py:15
  29.6 245.3 %collective-permute-start.3 = (bf16[32,32,512]{2,1,0:T(8,128)(2,1)}, bf16[32,32,512]{2,1,0:T(8,128)(2,1)}, u32[]{:S(2)}, u32[]{:S(2)}) collective-permute-start(bf16[32,32,512]{2,1,0:T(8,128)(2,1)} %pad_maximum_fusion.2), channel_id=1, source_target_pairs={{16,0},{20,4},{24,8},{28,12},{32,16},{36,20},{40,24},{44,28},{48,3... | collective-permute-start | bytes 3145736 | tf_op jit(solution)/shard_map/ppermute | solution.py:15
  36.4 245.7 %collective-permute-start.4 = (bf16[32,32,512]{2,1,0:T(8,128)(2,1)}, bf16[32,32,512]{2,1,0:T(8,128)(2,1)}, u32[]{:S(2)}, u32[]{:S(2)}) collective-permute-start(bf16[32,32,512]{2,1,0:T(8,128)(2,1)} %pad_maximum_fusion.2), channel_id=1, source_target_pairs={{20,0},{24,4},{28,8},{32,12},{36,16},{40,20},{44,24},{48,28},{52,3... | collective-permute-start | bytes 3145736 | tf_op jit(solution)/shard_map/ppermute | solution.py:15
  55.4 234.1 %collective-permute-start.5 = (bf16[32,32,512]{2,1,0:T(8,128)(2,1)}, bf16[32,32,512]{2,1,0:T(8,128)(2,1)}, u32[]{:S(2)}, u32[]{:S(2)}) collective-permute-start(bf16[32,32,512]{2,1,0:T(8,128)(2,1)} %pad_maximum_fusion.2), channel_id=1, source_target_pairs={{24,0},{28,4},{32,8},{36,12},{40,16},{44,20},{48,24},{52,28},{56,3... | collective-permute-start | bytes 3145736 | tf_op jit(solution)/shard_map/ppermute | solution.py:15
  86.0 210.7 %collective-permute-start.6 = (bf16[32,32,512]{2,1,0:T(8,128)(2,1)}, bf16[32,32,512]{2,1,0:T(8,128)(2,1)}, u32[]{:S(2)}, u32[]{:S(2)}) collective-permute-start(bf16[32,32,512]{2,1,0:T(8,128)(2,1)} %pad_maximum_fusion.2), channel_id=1, source_target_pairs={{28,0},{32,4},{36,8},{40,12},{44,16},{48,20},{52,24},{56,28},{60,3... | collective-permute-start | bytes 3145736 | tf_op jit(solution)/shard_map/ppermute | solution.py:15
  157.1 147.1 %collective-permute-start.7 = (bf16[32,32,512]{2,1,0:T(8,128)(2,1)}, bf16[32,32,512]{2,1,0:T(8,128)(2,1)}, u32[]{:S(2)}, u32[]{:S(2)}) collective-permute-start(bf16[32,32,512]{2,1,0:T(8,128)(2,1)} %pad_maximum_fusion.2), channel_id=1, source_target_pairs={{32,0},{36,4},{40,8},{44,12},{48,16},{52,20},{56,24},{60,28},{64,3... | collective-permute-start | bytes 3145736 | tf_op jit(solution)/shard_map/ppermute | solution.py:15
  244.6 6.5 %copy-start.2 = (bf16[32,32,2,256]{1,0,2,3:T(8,128)(2,1)S(1)}, bf16[32,32,2,256]{1,0,2,3:T(8,128)(2,1)}, u32[]{:S(2)}) copy-start(bf16[32,32,2,256]{1,0,2,3:T(8,128)(2,1)} %copy.71) | copy-start | bytes 3145732
  388.3 8.0 %copy-start.3 = (bf16[32,32,1,256]{1,0,2,3:T(8,128)(2,1)S(1)}, bf16[32,32,1,256]{1,0,2,3:T(8,128)(2,1)}, u32[]{:S(2)}) copy-start(bf16[32,32,1,256]{1,0,2,3:T(8,128)(2,1)} %get-tuple-element.6) | copy-start | bytes 1572868
  433.9 4.6 copy-start.6
  456.4 86.6 %copy-start.1 = (bf16[32,32,512]{2,1,0:T(8,128)(2,1)S(1)}, bf16[32,32,512]{2,1,0:T(8,128)(2,1)}, u32[]{:S(2)}) copy-start(bf16[32,32,512]{2,1,0:T(8,128)(2,1)} %param.2) | copy-start | bytes 3145732
Sparse Core Ops, SparseCore 0:
  456.6 83.7 reduce-scatter.1
where the time goes:
time: 553 us; the launch traced here: 550 us
  waiting for transfers between devices  182 us (33%)
  local copies, waits for them, and re-layouts  178 us (32%)
  starting transfers between devices  116 us (21%)
  matrix products  43.9 us (8%)
  other arithmetic  16.5 us (3%)
  between operations  13.7 us (2%)
    ppermute x8, starting transfers between devices, from_behind(): lax.ppermute(value, axis, [(source, source + steps) for source in range(i...  116 us
    ppermute x8, waiting for transfers between devices, from_behind(): lax.ppermute(value, axis, [(source, source + steps) for source in range(i...  97.9 us
    concatenate x17, local copies, waits for them, and re-layouts, body(): band_window = jnp.concatenate(tile_list, axis=0)  96.6 us
    reduce_scatter x1, waiting for transfers between devices, body(): lax.psum_scatter(lag_transform(cross_real, cross_imag, half_length), 'tm'...  83.9 us
    dot_general x1, matrix products, lag_transform(): jnp.einsum('cok,kt->cot', both_parts, both_tables, precision=lax.Precisio...  17.9 us
    reshape x2, local copies, waits for them, and re-layouts, skew_cut_last(): skew_grid = flattened.reshape(row_count, col_width + 1, bin_width)  16 us
    pad x2, local copies, waits for them, and re-layouts, skew_cut_last(): flattened = jnp.pad(flattened, ((0, row_count), (0, 0)))  12.9 us
    dot_general x1, matrix products, cross_window(): jnp.einsum('cmpk,jmpk->cjk', rows_parts, cols_parts, preferred_element_ty...  12.7 us
  transfers between devices with their start and end apart: 9, of which 3 were waited for; matrix products, arithmetic and copies ran while one was open for 14% of the time, Pallas kernels for 0%

commit v1 on v0

v1 whole, which is shorter than its diff:
```python
import jax
import jax.numpy as jnp
import numpy as np
from jax import lax
from jax.experimental import pallas as pl
from jax.experimental.pallas import tpu as pltpu
from jax.sharding import PartitionSpec as P

NFFT = 512
HALF = 256
OFFS = 256
LAGS = 256
SMOOTH = 32
AXES = ("row", "col", "tm")
LANES = 128
VMEM_BYTES = 48 * 1024 * 1024


def dft_table_t():
    n = np.arange(NFFT, dtype=np.float64)[None, :]
    k = np.arange(HALF, dtype=np.float64)[:, None]
    taper = 0.5 - 0.5 * np.cos(2.0 * np.pi * n / NFFT)
    phase = 2.0 * np.pi * np.mod(n * k, NFFT) / NFFT
    return np.concatenate([taper * np.cos(phase), -taper * np.sin(phase)], axis=0).astype(jnp.bfloat16)


def band_tables():
    k = np.arange(HALF)
    band = (np.abs(k[:, None] - k[None, :]) <= SMOOTH).astype(np.float32)
    inverse = np.broadcast_to(1.0 / band.sum(axis=1, keepdims=True), (HALF, LANES))
    return band.astype(jnp.bfloat16), inverse.astype(np.float32)


def lag_table():
    k = np.arange(HALF, dtype=np.float64)[:, None]
    t = (np.arange(LAGS) - LAGS // 2).astype(np.float64)[None, :]
    weight = np.where(k == 0, 1.0, 2.0) / NFFT
    phase = 2.0 * np.pi * np.mod(k * t, NFFT) / NFFT
    return np.concatenate([weight * np.cos(phase), -weight * np.sin(phase)], axis=0).astype(jnp.bfloat16)


def whiten_kernel(traces_ref, live_ref, table_ref, band_ref, inverse_ref, out_ref, scratch):
    table = table_ref[...]
    band = band_ref[...]
    inverse = inverse_ref[...]
    for pair in range(4):
        rows = jnp.concatenate(
            [traces_ref[high, 2 * pair + low] for low in range(2) for high in range(4)], axis=0
        )
        spectra = lax.dot_general(
            table, rows, (((1,), (1,)), ((), ())), preferred_element_type=jnp.float32
        )
        real, imag = spectra[:HALF], spectra[HALF:]
        power = real * real + imag * imag
        power_high = power.astype(jnp.bfloat16)
        power_low = (power - power_high.astype(jnp.float32)).astype(jnp.bfloat16)
        total = jnp.dot(band, power_high, preferred_element_type=jnp.float32) + jnp.dot(
            band, power_low, preferred_element_type=jnp.float32
        )
        for low in range(2):
            lanes = slice(low * LANES, (low + 1) * LANES)
            channel_low = 2 * pair + low
            smoothed = total[:, lanes] * inverse
            amplitude = live_ref[channel_low : channel_low + 1, :] * lax.rsqrt(smoothed + 1e-06)
            scratch[pl.ds(channel_low, HALF, stride=16), :] = real[:, lanes] * amplitude
            scratch[pl.ds(8 + channel_low, HALF, stride=16), :] = imag[:, lanes] * amplitude
    out_ref[...] = scratch[...].astype(jnp.bfloat16)


def cross_kernel(received_ref, flip_ref, out_ref, window):
    tiles = received_ref.shape[0]
    channels = tiles * 32
    lane_block = lax.broadcasted_iota(jnp.int32, (16, LANES), 1) // 32
    odd = lane_block % 2 == 1
    upper = lane_block >= 2
    window[pl.ds(channels, OFFS), :] = jnp.zeros((OFFS, 2 * LANES), jnp.bfloat16)

    def place(tile, carry):
        block = [received_ref[tile, source].astype(jnp.float32) for source in range(4)]
        step = []
        for first in (0, 2):
            step.append(jnp.where(odd, pltpu.roll(block[first + 1], 32, 1), block[first]))
            step.append(jnp.where(odd, block[first + 1], pltpu.roll(block[first], 96, 1)))
        by_high = [None] * 4
        for first in (0, 1):
            by_high[first] = jnp.where(upper, pltpu.roll(step[first + 2], 64, 1), step[first])
            by_high[first + 2] = jnp.where(upper, step[first + 2], pltpu.roll(step[first], 64, 1))
        for part in range(2):
            rows = jnp.concatenate([high[8 * part : 8 * part + 8] for high in by_high], axis=0)
            window[pl.ds(pl.multiple_of(tile * 32, 32), 32), part * LANES : (part + 1) * LANES] = (
                rows.astype(jnp.bfloat16)
            )
        return carry

    lax.fori_loop(0, tiles, place, 0, unroll=4)
    flip = flip_ref[...]

    def product(index, carry):
        start = pl.multiple_of(index * LANES, LANES)
        own = jnp.dot(flip, window[pl.ds(start, LANES), :], preferred_element_type=jnp.float32)
        real, imag = own[:, :LANES], own[:, LANES:]
        others = window[pl.ds(start, LANES + OFFS), :]
        for part, rows in enumerate(((real, imag), (imag, -real))):
            rows = jnp.concatenate(rows, axis=1).astype(jnp.bfloat16)
            cross = lax.dot_general(
                rows, others, (((1,), (1,)), ((), ())), preferred_element_type=jnp.float32
            )
            cross = pltpu.roll(cross, OFFS, 1, stride=1, stride_axis=0)
            for group in range(16):
                eight = cross[8 * group : 8 * group + 8]
                both = jnp.concatenate([eight[:, :LANES], eight[:, LANES : 2 * LANES]], axis=0)
                out_ref[index * 16 + 15 - group, part] = both.astype(jnp.bfloat16)
        return carry

    lax.fori_loop(0, channels // LANES, product, 0)


def lag_kernel(received_ref, table_ref, out_ref, scratch):
    scratch[...] = received_ref[...].astype(jnp.float32)
    table = table_ref[...]
    for channel in range(8):
        for upper in range(2):
            first = upper * 8 + 7 - channel
            real = scratch[pl.ds(first, HALF, stride=32), :]
            imag = scratch[pl.ds(16 + first, HALF, stride=32), :]
            both = jnp.concatenate([real, imag], axis=0).astype(jnp.bfloat16)
            lags = lax.dot_general(
                both, table, (((0,), (0,)), ((), ())), preferred_element_type=jnp.float32
            )
            out_ref[channel, upper * LANES : (upper + 1) * LANES, :] = lags.astype(jnp.bfloat16)


def call(kernel, shape, dtype, scratch):
    return pl.pallas_call(
        kernel,
        out_shape=jax.ShapeDtypeStruct(shape, dtype),
        scratch_shapes=[scratch],
        compiler_params=pltpu.CompilerParams(vmem_limit_bytes=VMEM_BYTES),
    )


def body(traces, live_flags):
    live = jnp.repeat(live_flags.astype(jnp.float32).reshape(4, 8).T, 32, axis=1)
    band, inverse = band_tables()
    whitened = call(
        whiten_kernel, (HALF * 16, LANES), jnp.bfloat16, pltpu.VMEM((HALF * 16, LANES), jnp.float32)
    )(traces.reshape(4, 8, 32, NFFT), live, jnp.asarray(dft_table_t()), jnp.asarray(band), jnp.asarray(inverse))
    one_bin = lax.all_to_all(whitened.reshape(HALF, 16, LANES), AXES, 0, 0, tiled=True)

    flip = np.eye(LANES, dtype=np.float32)[::-1].astype(jnp.bfloat16)
    cross = call(
        cross_kernel, (HALF, 2, 16, LANES), jnp.bfloat16, pltpu.VMEM((2048 + OFFS, 2 * LANES), jnp.bfloat16)
    )(one_bin.reshape(64, 4, 16, LANES), jnp.asarray(flip))
    all_bins = lax.all_to_all(cross.reshape(HALF, 32, LANES), AXES, 0, 0, tiled=True)

    return call(
        lag_kernel, (8, OFFS, LAGS), jnp.bfloat16, pltpu.VMEM((HALF * 32, LANES), jnp.float32)
    )(all_bins.reshape(HALF * 32, LANES), jnp.asarray(lag_table()))


def solution(mesh):
    return jax.shard_map(
        body,
        mesh=mesh,
        in_specs=(P(("row", "col"), "tm", None), P(("row", "col"))),
        out_specs=P(AXES, None, None),
        check_vma=False,
    )
```

time: 553 us -> 127 us (0.23)
  waiting for transfers between devices: 182 us -> 0 us
  local copies, waits for them, and re-layouts: 178 us -> 4.42 us
  starting transfers between devices: 116 us -> 0 us
  blocking collectives: 0 us -> 105 us
  matrix products: 43.9 us -> 0 us
  Pallas kernels: 0 us -> 16.3 us
  other arithmetic: 16.5 us -> 0.66 us
  between operations: 13.7 us -> 0.03 us
    ppermute x8 -> x0, starting transfers between devices: 116 us -> none  [from_behind(): lax.ppermute(value, axis, [(source, source + steps) for source in range(i...]
    all_to_all x0 -> x2, blocking collectives: none -> 105 us  [the longest x1 59.4 us: body(): lax.all_to_all(cross.reshape(HALF, 32, LANES), AXES, 0, 0, tiled=True)]
    concatenate x20 -> x0, local copies, waits for them, and re-layouts: 105 us -> none  [the longest x17 96.6 us: body(): band_window = jnp.concatenate(tile_list, axis=0)]
    ppermute x8 -> x0, waiting for transfers between devices: 97.9 us -> none  [from_behind(): lax.ppermute(value, axis, [(source, source + steps) for source in range(i...]
    reduce_scatter x1 -> x0, waiting for transfers between devices: 83.9 us -> none  [body(): lax.psum_scatter(lag_transform(cross_real, cross_imag, half_length), 'tm'...]
    dot_general x5 -> x0, matrix products: 43.9 us -> none  [the longest x1 17.9 us: lag_transform(): jnp.einsum('cok,kt->cot', both_parts, both_tables, precision=lax.Precisio...]
    transpose x2 -> x1, local copies, waits for them, and re-layouts: 23.4 us -> 0.08 us  [body(): live_flags.astype(jnp.float32).reshape(4, 8)]
    pallas_call x0 -> x3, Pallas kernels: none -> 16.3 us  [the longest x1 9.78 us: body(): call(cross_kernel, (HALF, 2, 16, LANES), jnp.bfloat16, pltpu.VMEM((2048 +...]
  transfers between devices with their start and end apart: 9 -> 0, of which waited for: 3 -> 0; matrix products, arithmetic and copies ran while one was open for 14% -> 0% of each run, Pallas kernels for 0% -> 0%
where the time goes in v1:
time: 127 us; the launch traced here: 126 us
  blocking collectives  105 us (83%)
  Pallas kernels  16.3 us (13%)
  local copies, waits for them, and re-layouts  4.42 us (3%)
    all_to_all x1, blocking collectives, body(): lax.all_to_all(cross.reshape(HALF, 32, LANES), AXES, 0, 0, tiled=True)  59.4 us
    all_to_all x1, blocking collectives, body(): lax.all_to_all(whitened.reshape(HALF, 16, LANES), AXES, 0, 0, tiled=True)  45.8 us
    pallas_call x1, Pallas kernels, body(): call(cross_kernel, (HALF, 2, 16, LANES), jnp.bfloat16, pltpu.VMEM((2048 +...  9.78 us
    unnamed x12, local copies, waits for them, and re-layouts  4.09 us
    pallas_call x1, Pallas kernels, body(): call(lag_kernel, (8, OFFS, LAGS), jnp.bfloat16, pltpu.VMEM((HALF * 32, LA...  3.9 us
    pallas_call x1, Pallas kernels, body(): call(whiten_kernel, (HALF * 16, LANES), jnp.bfloat16, pltpu.VMEM((HALF *...  2.59 us

profile of v1, /device:TPU:1, one launch (start us, length us, event | category | flops | bytes accessed | tf_op | source)
XLA Modules:
  0.0 126.5 jit_solution(15167344441934175662)
XLA Ops:
  0.0 0.7 convert_element_type.3
  0.7 0.1 reshape.22
  0.7 0.1 copy.8
  0.8 0.1 broadcast_in_dim.3
  0.9 0.1 reshape.23.live_ref
  1.0 0.0 copy-start
  1.0 1.2 copy-done
  2.2 0.0 copy-start.1
  2.2 1.0 copy-done.1
  3.3 0.0 copy-start.3
  3.3 0.9 copy-done.3
  4.2 0.0 copy-start.4
  4.2 0.9 copy-done.4
  5.1 0.0 copy-start.5
  5.1 2.6 %shard_map.73 = bf16[4096,128]{1,0:T(8,128)(2,1)S(1)} custom-call(bf16[4,8,32,512]{3,2,1,0:T(8,128)(2,1)S(1)} %bitcast.10, f32[8,128]{1,0:T(8,128)S(1)} %reshape.23.live_ref, bf16[512,512]{1,0:T(8,128)(2,1)S(1)} %copy-done.1, bf16[256,256]{1,0:T(8,128)(2,1)S(1)} %copy-done.4, f32[256,128]{1,0:T(8,128)S(1)} %copy-done.3), custom_call_target="tpu_custom_call" | custom-call | tf_op jit(solution)/shard_map/pallas_call | solution.py:145
  7.7 45.8 %all_to_all.10 = bf16[256,16,128]{2,1,0:T(8,128)(2,1)S(1)} all-to-all(bf16[256,16,128]{2,1,0:T(8,128)(2,1)S(1)} %bitcast.9), channel_id=1, replica_groups=mesh['row'=4,'col'=16,'tm'=4] {'row','col','tm'}, dimensions={0} | all-to-all | bytes 2097152 | tf_op jit(solution)/shard_map/all_to_all | solution.py:148
  53.4 0.0 copy-done.5
  53.4 9.8 %shard_map.74 = bf16[256,2,16,128]{3,2,1,0:T(8,128)(2,1)S(1)} custom-call(bf16[64,4,16,128]{3,2,1,0:T(8,128)(2,1)S(1)} %bitcast.8, bf16[128,128]{1,0:T(8,128)(2,1)S(1)} %copy-done.5), custom_call_target="tpu_custom_call" | custom-call | tf_op jit(solution)/shard_map/pallas_call | solution.py:151
  63.2 0.0 copy-start.2
  63.2 59.4 %all_to_all.11 = bf16[256,32,128]{2,1,0:T(8,128)(2,1)S(1)} all-to-all(bf16[256,32,128]{2,1,0:T(8,128)(2,1)S(1)} %bitcast.6), channel_id=1, replica_groups=mesh['row'=4,'col'=16,'tm'=4] {'row','col','tm'}, dimensions={0} | all-to-all | bytes 4194304 | tf_op jit(solution)/shard_map/all_to_all | solution.py:154
  122.6 0.0 copy-done.2
  122.6 3.9 %shard_map.75 = bf16[8,256,256]{2,1,0:T(8,128)(2,1)} custom-call(bf16[8192,128]{1,0:T(8,128)(2,1)S(1)} %bitcast.7, bf16[512,256]{1,0:T(8,128)(2,1)S(1)} %copy-done.2), custom_call_target="tpu_custom_call" | custom-call | tf_op jit(solution)/shard_map/pallas_call | solution.py:156
Async XLA Ops:
  1.0 1.2 copy-start
  2.2 1.0 copy-start.1
  3.3 0.9 copy-start.3
  4.2 0.9 copy-start.4
  5.1 48.4 %copy-start.5 = (bf16[128,128]{1,0:T(8,128)(2,1)S(1)}, bf16[128,128]{1,0:T(8,128)(2,1)}, u32[]{:S(2)}) copy-start(bf16[128,128]{1,0:T(8,128)(2,1)} %constant.13.clone.flip_ref) | copy-start | bytes 98308
  63.2 59.4 %copy-start.2 = (bf16[512,256]{1,0:T(8,128)(2,1)S(1)}, bf16[512,256]{1,0:T(8,128)(2,1)}, u32[]{:S(2)}) copy-start(bf16[512,256]{1,0:T(8,128)(2,1)} %constant.14.clone.table_ref) | copy-start | bytes 786436

commit v2 on v1

v2 whole, which is shorter than its diff:
```python
import jax
import jax.numpy as jnp
import numpy as np
from jax import lax
from jax.experimental import pallas as pl
from jax.experimental.pallas import tpu as pltpu
from jax.sharding import PartitionSpec as P

NFFT = 512
HALF = 256
OFFS = 256
LAGS = 256
SMOOTH = 32
CHANNELS = 2048
TILES = 64
AXES = ("row", "col", "tm")
LANES = 128
MIB = 1024 * 1024


def dft_table_t():
    n = np.arange(NFFT, dtype=np.float64)[None, :]
    k = np.arange(HALF, dtype=np.float64)[:, None]
    taper = 0.5 - 0.5 * np.cos(2.0 * np.pi * n / NFFT)
    phase = 2.0 * np.pi * np.mod(n * k, NFFT) / NFFT
    return np.concatenate([taper * np.cos(phase), -taper * np.sin(phase)], axis=0).astype(jnp.bfloat16)


def lag_table():
    k = np.arange(HALF, dtype=np.float64)[:, None]
    t = (np.arange(LAGS) - LAGS // 2).astype(np.float64)[None, :]
    weight = np.where(k == 0, 1.0, 2.0) / NFFT
    phase = 2.0 * np.pi * np.mod(k * t, NFFT) / NFFT
    return np.concatenate([weight * np.cos(phase), -weight * np.sin(phase)], axis=0).astype(jnp.bfloat16)


def zero_one(shape, holds):
    row = lax.broadcasted_iota(jnp.int32, shape, 0)
    column = lax.broadcasted_iota(jnp.int32, shape, 1)
    return jnp.where(holds(row, column), 1.0, 0.0).astype(jnp.bfloat16)


def product(left, right):
    return jnp.dot(left, right, preferred_element_type=jnp.float32)


def product_nt(left, right):
    return lax.dot_general(left, right, (((1,), (1,)), ((), ())), preferred_element_type=jnp.float32)


def whiten_kernel(flags_ref, traces_ref, table_ref, out_ref, scratch):
    band = zero_one((HALF, 2 * HALF), lambda r, c: jnp.abs(r - c % HALF) <= SMOOTH)
    bin_index = lax.broadcasted_iota(jnp.int32, (HALF, LANES), 0)
    count = jnp.minimum(bin_index + SMOOTH, HALF - 1) - jnp.maximum(bin_index - SMOOTH, 0) + 1
    inverse = 1.0 / count.astype(jnp.float32)
    lane_block = lax.broadcasted_iota(jnp.int32, (1, LANES), 1) // 32
    table = table_ref[...]
    width = 4
    for start in range(0, 8, width):
        rows = jnp.concatenate(
            [traces_ref[high, start + low] for low in range(width) for high in range(4)], axis=0
        )
        spectra = product_nt(table, rows)
        real, imag = spectra[:HALF], spectra[HALF:]
        power = real * real + imag * imag
        power_high = power.astype(jnp.bfloat16)
        power_low = (power - power_high.astype(jnp.float32)).astype(jnp.bfloat16)
        total = product(band, jnp.concatenate([power_high, power_low], axis=0))
        for low in range(width):
            lanes = slice(low * LANES, (low + 1) * LANES)
            channel_low = start + low
            live = jnp.zeros((1, LANES), jnp.float32)
            for high in range(4):
                live = jnp.where(lane_block == high, flags_ref[high * 8 + channel_low].astype(jnp.float32), live)
            amplitude = live * lax.rsqrt(total[:, lanes] * inverse + 1e-06)
            scratch[pl.ds(channel_low, HALF, stride=16), :] = real[:, lanes] * amplitude
            scratch[pl.ds(8 + channel_low, HALF, stride=16), :] = imag[:, lanes] * amplitude
    out_ref[...] = scratch[...].astype(jnp.bfloat16)


def cross_kernel(received_ref, out_ref, window):
    window[CHANNELS:, :] = jnp.zeros((OFFS, 2 * LANES), jnp.bfloat16)
    swap = zero_one(
        (4 * LANES, 4 * LANES),
        lambda r, c: (r % 32 == c % 32) & (r // 32 % 4 == c // 128) & (r // 128 == c // 32 % 4),
    )
    group = 16
    for first in range(0, TILES, group):
        side_by_side = jnp.concatenate(
            [received_ref[first : first + group, block].reshape(group * 16, LANES) for block in range(4)], axis=1
        )
        swapped = product(side_by_side, swap)
        for tile in range(group):
            for part in range(2):
                eight = swapped[tile * 16 + part * 8 : tile * 16 + part * 8 + 8]
                rows = jnp.concatenate([eight[:, high * LANES : (high + 1) * LANES] for high in range(4)], axis=0)
                start = (first + tile) * 32
                window[start : start + 32, part * LANES : (part + 1) * LANES] = rows.astype(jnp.bfloat16)

    flip = zero_one((LANES, LANES), lambda r, c: r + c == LANES - 1)

    def step(index, carry):
        start = pl.multiple_of(index * LANES, LANES)
        own = product(flip, window[pl.ds(start, LANES), :])
        real, imag = own[:, :LANES], own[:, LANES:]
        others = window[pl.ds(start, LANES + OFFS), :]
        rows = jnp.concatenate(
            [jnp.concatenate([real, imag], axis=1), jnp.concatenate([imag, -real], axis=1)], axis=0
        ).astype(jnp.bfloat16)
        both_parts = product_nt(rows, others)
        for part in range(2):
            cross = both_parts[part * LANES : (part + 1) * LANES]
            cross = pltpu.roll(cross, OFFS, 1, stride=1, stride_axis=0)
            for place in range(16):
                eight = cross[8 * place : 8 * place + 8]
                halves = jnp.concatenate([eight[:, :LANES], eight[:, LANES : 2 * LANES]], axis=0)
                out_ref[index * 16 + 15 - place, part] = halves.astype(jnp.bfloat16)
        return carry

    steps = CHANNELS // LANES
    lax.fori_loop(0, steps, step, 0, unroll=steps)


def lag_kernel(received_ref, table_ref, out_ref, lags, sems):
    table = table_ref[...]
    copies = []
    for channel in range(8):
        columns = []
        for upper in range(2):
            first = upper * 8 + 7 - channel
            real = received_ref[pl.ds(first, HALF, stride=32), :]
            imag = received_ref[pl.ds(16 + first, HALF, stride=32), :]
            columns.append(jnp.concatenate([real, imag], axis=0))
        both = jnp.concatenate(columns, axis=1)
        lags[channel] = lax.dot_general(
            both, table, (((0,), (0,)), ((), ())), preferred_element_type=jnp.float32
        ).astype(jnp.bfloat16)
        copy = pltpu.make_async_copy(lags.at[channel], out_ref.at[channel], sems.at[channel])
        copy.start()
        copies.append(copy)
    for copy in copies:
        copy.wait()


def call(kernel, shape, scratch, vmem_mib, **specs):
    return pl.pallas_call(
        kernel,
        out_shape=jax.ShapeDtypeStruct(shape, jnp.bfloat16),
        scratch_shapes=scratch,
        compiler_params=pltpu.CompilerParams(vmem_limit_bytes=vmem_mib * MIB),
        **specs,
    )


def body(traces, live_flags):
    vmem = pl.BlockSpec(memory_space=pltpu.VMEM)
    whitened = call(
        whiten_kernel,
        (HALF * 16, LANES),
        [pltpu.VMEM((HALF * 16, LANES), jnp.float32)],
        63,
        in_specs=[pl.BlockSpec(memory_space=pltpu.SMEM), vmem, vmem],
    )(live_flags, traces.reshape(4, 8, 32, NFFT), jnp.asarray(dft_table_t()))
    one_bin = lax.all_to_all(whitened.reshape(HALF, 16, LANES), AXES, 0, 0, tiled=True)

    cross = call(
        cross_kernel,
        (HALF, 2, 16, LANES),
        [pltpu.VMEM((CHANNELS + OFFS, 2 * LANES), jnp.bfloat16)],
        40,
    )(one_bin.reshape(TILES, 4, 16, LANES))
    all_bins = lax.all_to_all(cross.reshape(HALF, 32, LANES), AXES, 0, 0, tiled=True)

    return call(
        lag_kernel,
        (8, OFFS, LAGS),
        [pltpu.VMEM((8, OFFS, LAGS), jnp.bfloat16), pltpu.SemaphoreType.DMA((8,))],
        40,
        in_specs=[vmem, vmem],
        out_specs=pl.BlockSpec(memory_space=pltpu.HBM),
    )(all_bins.reshape(HALF * 32, LANES), jnp.asarray(lag_table()))


def solution(mesh):
    return jax.shard_map(
        body,
        mesh=mesh,
        in_specs=(P(("row", "col"), "tm", None), P(("row", "col"))),
        out_specs=P(AXES, None, None),
        check_vma=False,
    )
```

time: 127 us -> 117 us (0.921)
  Pallas kernels: 16.3 us -> 11.8 us
  local copies, waits for them, and re-layouts: 4.42 us -> 0.01 us
    pallas_call x3, Pallas kernels: 16.3 us -> 11.8 us  [the longest x1 4.29 us: body(): call(whiten_kernel, (HALF * 16, LANES), [pltpu.VMEM((HALF * 16, LANES), j...]
    unnamed x12 -> x2, local copies, waits for them, and re-layouts: 4.09 us -> 0.01 us
where the time goes in v2:
time: 117 us
  blocking collectives  105 us (90%)
  Pallas kernels  11.8 us (10%)
    all_to_all x1, blocking collectives, body(): lax.all_to_all(cross.reshape(HALF, 32, LANES), AXES, 0, 0, tiled=True)  59.4 us
    all_to_all x1, blocking collectives, body(): lax.all_to_all(whitened.reshape(HALF, 16, LANES), AXES, 0, 0, tiled=True)  46 us
    pallas_call x1, Pallas kernels, body(): call(whiten_kernel, (HALF * 16, LANES), [pltpu.VMEM((HALF * 16, LANES), j...  4.29 us
    pallas_call x1, Pallas kernels, body(): call(cross_kernel, (HALF, 2, 16, LANES), [pltpu.VMEM((CHANNELS + OFFS, 2...  4.2 us
    pallas_call x1, Pallas kernels, body(): call(lag_kernel, (8, OFFS, LAGS), [pltpu.VMEM((8, OFFS, LAGS), jnp.bfloat...  3.28 us

profile of v2, /device:TPU:1, one launch (start us, length us, event | category | flops | bytes accessed | tf_op | source)
XLA Modules:
  0.0 117.1 jit_solution(10227927651132712460)
XLA Ops:
  0.0 4.3 %shard_map.46 = bf16[4096,128]{1,0:T(8,128)(2,1)} custom-call(s32[32]{0:T(128)} %flags_ref.1, bf16[4,8,32,512]{3,2,1,0:T(8,128)(2,1)} %bitcast.9, bf16[512,512]{1,0:T(8,128)(2,1)} %constant.4.clone.table_ref), custom_call_target="tpu_custom_call" | custom-call | tf_op jit(solution)/shard_map/pallas_call | solution.py:157
  4.3 46.0 %all_to_all.10 = bf16[256,16,128]{2,1,0:T(8,128)(2,1)S(1)} all-to-all(bf16[256,16,128]{2,1,0:T(8,128)(2,1)} %bitcast.8), channel_id=1, replica_groups=mesh['row'=4,'col'=16,'tm'=4] {'row','col','tm'}, dimensions={0} | all-to-all | bytes 2097152 | tf_op jit(solution)/shard_map/all_to_all | solution.py:164
  50.3 4.2 %shard_map.47 = bf16[256,2,16,128]{3,2,1,0:T(8,128)(2,1)S(1)} custom-call(bf16[64,4,16,128]{3,2,1,0:T(8,128)(2,1)S(1)} %bitcast.7), custom_call_target="tpu_custom_call" | custom-call | tf_op jit(solution)/shard_map/pallas_call | solution.py:166
  54.5 0.0 copy-start
  54.5 59.4 %all_to_all.11 = bf16[256,32,128]{2,1,0:T(8,128)(2,1)S(1)} all-to-all(bf16[256,32,128]{2,1,0:T(8,128)(2,1)S(1)} %bitcast.6), channel_id=1, replica_groups=mesh['row'=4,'col'=16,'tm'=4] {'row','col','tm'}, dimensions={0} | all-to-all | bytes 4194304 | tf_op jit(solution)/shard_map/all_to_all | solution.py:172
  113.8 0.0 copy-done
  113.8 3.3 %shard_map.48 = bf16[8,256,256]{2,1,0:T(8,128)(2,1)} custom-call(bf16[8192,128]{1,0:T(8,128)(2,1)S(1)} %bitcast.5, bf16[512,256]{1,0:T(8,128)(2,1)S(1)} %copy-done), custom_call_target="tpu_custom_call" | custom-call | tf_op jit(solution)/shard_map/pallas_call | solution.py:174
Async XLA Ops:
  54.5 59.4 %copy-start = (bf16[512,256]{1,0:T(8,128)(2,1)S(1)}, bf16[512,256]{1,0:T(8,128)(2,1)}, u32[]{:S(2)}) copy-start(bf16[512,256]{1,0:T(8,128)(2,1)} %constant.5.clone.table_ref) | copy-start | bytes 786436

commit v3 on v2

v3 whole, which is shorter than its diff:
```python
import jax
import jax.numpy as jnp
import numpy as np
from jax import lax
from jax.experimental import pallas as pl
from jax.experimental.pallas import tpu as pltpu
from jax.sharding import PartitionSpec as P

NFFT = 512
HALF = 256
OFFS = 256
LAGS = 256
SMOOTH = 32
AXES = ("row", "col", "tm")
GROUP_AXES = ("col", "tm")
GROUP = 64
BINS = HALF // GROUP
ROW = 512
LANES = 128
MIB = 1024 * 1024


def dft_table_t():
    n = np.arange(NFFT, dtype=np.float64)[None, :]
    k = np.arange(HALF, dtype=np.float64)[:, None]
    taper = 0.5 - 0.5 * np.cos(2.0 * np.pi * n / NFFT)
    phase = 2.0 * np.pi * np.mod(n * k, NFFT) / NFFT
    return np.concatenate([taper * np.cos(phase), -taper * np.sin(phase)], axis=0).astype(jnp.bfloat16)


def lag_table():
    k = np.arange(HALF, dtype=np.float64)[:, None]
    t = (np.arange(LAGS) - LAGS // 2).astype(np.float64)[None, :]
    weight = np.where(k == 0, 1.0, 2.0) / NFFT
    phase = 2.0 * np.pi * np.mod(k * t, NFFT) / NFFT
    return np.concatenate([weight * np.cos(phase), -weight * np.sin(phase)], axis=0).astype(jnp.bfloat16)


def zero_one(shape, holds):
    row = lax.broadcasted_iota(jnp.int32, shape, 0)
    column = lax.broadcasted_iota(jnp.int32, shape, 1)
    return jnp.where(holds(row, column), 1.0, 0.0).astype(jnp.bfloat16)


def product(left, right):
    return jnp.dot(left, right, preferred_element_type=jnp.float32)


def product_nt(left, right):
    return lax.dot_general(left, right, (((1,), (1,)), ((), ())), preferred_element_type=jnp.float32)


def whiten_kernel(flags_ref, traces_ref, table_ref, out_ref, scratch, rounded, sems):
    band = zero_one((HALF, 2 * HALF), lambda r, c: jnp.abs(r - c % HALF) <= SMOOTH)
    bin_index = lax.broadcasted_iota(jnp.int32, (HALF, LANES), 0)
    count = jnp.minimum(bin_index + SMOOTH, HALF - 1) - jnp.maximum(bin_index - SMOOTH, 0) + 1
    inverse = 1.0 / count.astype(jnp.float32)
    lane_block = lax.broadcasted_iota(jnp.int32, (1, LANES), 1) // 32
    table = table_ref[...]
    width = 8
    for start in range(0, 8, width):
        rows = jnp.concatenate(
            [traces_ref[high, start + low] for low in range(width) for high in range(4)], axis=0
        )
        spectra = product_nt(table, rows)
        real, imag = spectra[:HALF], spectra[HALF:]
        power = real * real + imag * imag
        power_high = power.astype(jnp.bfloat16)
        power_low = (power - power_high.astype(jnp.float32)).astype(jnp.bfloat16)
        total = product(band, jnp.concatenate([power_high, power_low], axis=0))
        for low in range(width):
            lanes = slice(low * LANES, (low + 1) * LANES)
            channel_low = start + low
            live = jnp.zeros((1, LANES), jnp.float32)
            for high in range(4):
                live = jnp.where(lane_block == high, flags_ref[high * 8 + channel_low].astype(jnp.float32), live)
            amplitude = live * lax.rsqrt(total[:, lanes] * inverse + 1e-06)
            scratch[pl.ds(channel_low, HALF, stride=16), :] = real[:, lanes] * amplitude
            scratch[pl.ds(8 + channel_low, HALF, stride=16), :] = imag[:, lanes] * amplitude
    copies = []
    rows = HALF * 4
    for piece in range(4):
        part = pl.ds(piece * rows, rows)
        rounded[part, :] = scratch[part, :].astype(jnp.bfloat16)
        copies.append(pltpu.make_async_copy(rounded.at[part], out_ref.at[part], sems.at[piece]))
        copies[-1].start()
    for copy in copies:
        copy.wait()


def swap_table():
    r = np.arange(4 * LANES)[:, None]
    c = np.arange(4 * LANES)[None, :]
    same = (r % 32 == c % 32) & (r // 32 % 4 == c // 128) & (r // 128 == c // 32 % 4)
    return same.astype(np.float32).astype(jnp.bfloat16)


def flip_table():
    return np.eye(LANES, dtype=np.float32)[::-1].astype(jnp.bfloat16)


def place_tiles(received_ref, swap, index, window, first_row):
    tiles = received_ref.shape[0]
    side_by_side = jnp.concatenate(
        [received_ref[:, block, index].reshape(tiles * 16, LANES) for block in range(4)], axis=1
    )
    swapped = product(side_by_side, swap)
    for tile in range(tiles):
        for part in range(2):
            eight = swapped[tile * 16 + part * 8 : tile * 16 + part * 8 + 8]
            rows = jnp.concatenate([eight[:, high * LANES : (high + 1) * LANES] for high in range(4)], axis=0)
            start = first_row + tile * 32
            window[index, start : start + 32, part * LANES : (part + 1) * LANES] = rows.astype(jnp.bfloat16)


def cross_block(window, index, start, flip, out_ref, first_place):
    own = product(flip, window[index, start : start + LANES, :])
    real, imag = own[:, :LANES], own[:, LANES:]
    others = window[index, start : start + LANES + OFFS, :]
    rows = jnp.concatenate(
        [jnp.concatenate([real, imag], axis=1), jnp.concatenate([imag, -real], axis=1)], axis=0
    ).astype(jnp.bfloat16)
    both_parts = product_nt(rows, others)
    for part in range(2):
        cross = both_parts[part * LANES : (part + 1) * LANES]
        cross = pltpu.roll(cross, OFFS, 1, stride=1, stride_axis=0)
        for place in range(16):
            eight = cross[8 * place : 8 * place + 8]
            halves = jnp.concatenate([eight[:, :LANES], eight[:, LANES : 2 * LANES]], axis=0)
            out_ref[first_place + 15 - place, index, part] = halves.astype(jnp.bfloat16)


def near_kernel(received_ref, swap_ref, flip_ref, out_ref, rest_ref, window):
    swap = swap_ref[...]
    flip = flip_ref[...]
    half = window.shape[1] // 2
    for index in range(BINS):
        place_tiles(received_ref, swap, index, window, 0)
        rest_ref[index] = window[index, half:]
        for start in range(0, half, LANES):
            cross_block(window, index, start, flip, out_ref, start // 8)


def far_kernel(halo_ref, rest_ref, swap_ref, flip_ref, cross_ref, out_ref, window, results, sems):
    del cross_ref
    swap = swap_ref[...]
    flip = flip_ref[...]
    half = rest_ref.shape[1]
    places = half // 8
    copies = []
    for index in range(BINS):
        window[index, :half] = rest_ref[index]
        place_tiles(halo_ref, swap, index, window, half)
        for start in range(0, half, LANES):
            cross_block(window, index, start, flip, results, start // 8)
        copies.append(
            pltpu.make_async_copy(results.at[:, index], out_ref.at[pl.ds(places, places), index], sems.at[index])
        )
        copies[-1].start()
    for copy in copies:
        copy.wait()


def lag_kernel(received_ref, table_ref, out_ref, lags, sems):
    table = table_ref[...]
    copies = []
    for channel in range(8):
        columns = []
        for upper in range(2):
            first = upper * 8 + 7 - channel
            real = received_ref[pl.ds(first, HALF, stride=32), :]
            imag = received_ref[pl.ds(16 + first, HALF, stride=32), :]
            columns.append(jnp.concatenate([real, imag], axis=0))
        both = jnp.concatenate(columns, axis=1)
        lags[channel] = lax.dot_general(
            both, table, (((0,), (0,)), ((), ())), preferred_element_type=jnp.float32
        ).astype(jnp.bfloat16)
        if channel % 2:
            pair = pl.ds(channel - 1, 2)
            copies.append(pltpu.make_async_copy(lags.at[pair], out_ref.at[pair], sems.at[channel // 2]))
            copies[-1].start()
    for copy in copies:
        copy.wait()


def call(kernel, shape, scratch, vmem_mib, **options):
    return pl.pallas_call(
        kernel,
        out_shape=jax.tree.map(lambda s: jax.ShapeDtypeStruct(s, jnp.bfloat16), shape, is_leaf=lambda s: isinstance(s, tuple)),
        scratch_shapes=scratch,
        compiler_params=pltpu.CompilerParams(vmem_limit_bytes=vmem_mib * MIB),
        **options,
    )


def body(traces, live_flags):
    vmem = pl.BlockSpec(memory_space=pltpu.VMEM)
    hbm = pl.BlockSpec(memory_space=pltpu.HBM)
    anywhere = pl.BlockSpec(memory_space=pl.ANY)
    whitened = call(
        whiten_kernel,
        (HALF * 16, LANES),
        [
            pltpu.VMEM((HALF * 16, LANES), jnp.float32),
            pltpu.VMEM((HALF * 16, LANES), jnp.bfloat16),
            pltpu.SemaphoreType.DMA((4,)),
        ],
        63,
        in_specs=[pl.BlockSpec(memory_space=pltpu.SMEM), vmem, vmem],
        out_specs=hbm,
    )(live_flags, traces.reshape(4, 8, 32, NFFT), jnp.asarray(dft_table_t()))
    some_bins = lax.all_to_all(whitened.reshape(GROUP, BINS, 16, LANES), GROUP_AXES, 0, 0, tiled=True)
    some_bins = some_bins.reshape(ROW // 32, 4, BINS, 16, LANES)

    first = some_bins[: OFFS // 32]
    halo = lax.ppermute(first, "row", [(1, 0), (2, 1), (3, 2)])
    swap, flip = jnp.asarray(swap_table()), jnp.asarray(flip_table())
    cross, rest = call(
        near_kernel,
        [(GROUP, BINS, 2, 16, LANES), (BINS, ROW // 2, 2 * LANES)],
        [pltpu.VMEM((BINS, ROW, 2 * LANES), jnp.bfloat16)],
        32,
    )(some_bins, swap, flip)
    cross = call(
        far_kernel,
        (GROUP, BINS, 2, 16, LANES),
        [
            pltpu.VMEM((BINS, ROW // 2 + OFFS, 2 * LANES), jnp.bfloat16),
            pltpu.VMEM((GROUP // 2, BINS, 2, 16, LANES), jnp.bfloat16),
            pltpu.SemaphoreType.DMA((BINS,)),
        ],
        32,
        in_specs=[vmem, vmem, vmem, vmem, anywhere],
        out_specs=anywhere,
        input_output_aliases={4: 0},
    )(halo, rest, swap, flip, cross)
    all_bins = lax.all_to_all(cross.reshape(GROUP, BINS * 32, LANES), GROUP_AXES, 0, 0, tiled=True)

    return call(
        lag_kernel,
        (8, OFFS, LAGS),
        [pltpu.VMEM((8, OFFS, LAGS), jnp.bfloat16), pltpu.SemaphoreType.DMA((4,))],
        32,
        in_specs=[vmem, vmem],
        out_specs=hbm,
    )(all_bins.reshape(HALF * 32, LANES), jnp.asarray(lag_table()))


def solution(mesh):
    return jax.shard_map(
        body,
        mesh=mesh,
        in_specs=(P(("row", "col"), "tm", None), P(("row", "col"))),
        out_specs=P(AXES, None, None),
        check_vma=False,
    )
```

time: 117 us -> 115 us (0.983)
  blocking collectives: 105 us -> 91.3 us
  waiting for transfers between devices: 0 us -> 6.57 us
  starting transfers between devices: 0 us -> 4.33 us
    all_to_all x2, blocking collectives: 105 us -> 91.3 us  [the longest x1 51 us: body(): lax.all_to_all(cross.reshape(GROUP, BINS * 32, LANES), GROUP_AXES, 0, 0,...]
    ppermute x0 -> x1, waiting for transfers between devices: none -> 6.57 us  [body(): halo = lax.ppermute(first, 'row', [(1, 0), (2, 1), (3, 2)])]
    ppermute x0 -> x1, starting transfers between devices: none -> 4.33 us  [body(): halo = lax.ppermute(first, 'row', [(1, 0), (2, 1), (3, 2)])]
    pallas_call x1 -> x2, Pallas kernels: 4.2 us -> 5.88 us  [the longest x1 3.13 us: body(): call(far_kernel, (GROUP, BINS, 2, 16, LANES), [pltpu.VMEM((BINS, ROW // 2...]
  transfers between devices with their start and end apart: 0 -> 1, of which waited for: 0 -> 1; matrix products, arithmetic and copies ran while one was open for 0% -> 0% of each run, Pallas kernels for 0% -> 2%
where the time goes in v3:
time: 115 us; the launch traced here: 114 us
  blocking collectives  91.3 us (79%)
  Pallas kernels  12.1 us (11%)
  waiting for transfers between devices  6.57 us (6%)
  starting transfers between devices  4.33 us (4%)
    all_to_all x1, blocking collectives, body(): lax.all_to_all(cross.reshape(GROUP, BINS * 32, LANES), GROUP_AXES, 0, 0,...  51 us
    all_to_all x1, blocking collectives, body(): lax.all_to_all(whitened.reshape(GROUP, BINS, 16, LANES), GROUP_AXES, 0, 0...  40.3 us
    ppermute x1, waiting for transfers between devices, body(): halo = lax.ppermute(first, 'row', [(1, 0), (2, 1), (3, 2)])  6.57 us
    ppermute x1, starting transfers between devices, body(): halo = lax.ppermute(first, 'row', [(1, 0), (2, 1), (3, 2)])  4.33 us
    pallas_call x1, Pallas kernels, body(): call(whiten_kernel, (HALF * 16, LANES), [pltpu.VMEM((HALF * 16, LANES), j...  3.81 us
    pallas_call x1, Pallas kernels, body(): call(far_kernel, (GROUP, BINS, 2, 16, LANES), [pltpu.VMEM((BINS, ROW // 2...  3.13 us
    pallas_call x1, Pallas kernels, body(): call(near_kernel, [(GROUP, BINS, 2, 16, LANES), (BINS, ROW // 2, 2 * LANE...  2.76 us
    pallas_call x1, Pallas kernels, body(): call(lag_kernel, (8, OFFS, LAGS), [pltpu.VMEM((8, OFFS, LAGS), jnp.bfloat...  2.38 us
  transfers between devices with their start and end apart: 1, of which 1 were waited for; matrix products, arithmetic and copies ran while one was open for 0% of the time, Pallas kernels for 2%

profile of v3, /device:TPU:1, one launch (start us, length us, event | category | flops | bytes accessed | tf_op | source)
XLA Modules:
  0.0 114.4 jit_solution(4750437110757878740)
XLA Ops:
  0.0 3.8 %shard_map.64 = bf16[4096,128]{1,0:T(8,128)(2,1)} custom-call(s32[32]{0:T(128)} %flags_ref.1, bf16[4,8,32,512]{3,2,1,0:T(8,128)(2,1)} %bitcast.10, bf16[512,512]{1,0:T(8,128)(2,1)} %constant.8.clone.table_ref), custom_call_target="tpu_custom_call" | custom-call | tf_op jit(solution)/shard_map/pallas_call | solution.py:200
  3.8 0.0 copy-start
  3.8 0.0 copy-start.2
  3.8 40.3 %all_to_all.10 = bf16[64,4,16,128]{3,2,1,0:T(8,128)(2,1)S(1)} all-to-all(bf16[64,4,16,128]{3,2,1,0:T(8,128)(2,1)} %bitcast.9), channel_id=1, replica_groups=mesh['row'=4,'col'=16,'tm'=4] {'col','tm'}, dimensions={0} | all-to-all | bytes 2097152 | tf_op jit(solution)/shard_map/all_to_all | solution.py:212
  44.2 4.3 %collective-permute-start = (bf16[8,4,4,16,128]{4,3,2,1,0:T(8,128)(2,1)S(1)}, bf16[8,4,4,16,128]{4,3,2,1,0:T(8,128)(2,1)S(1)}, u32[]{:S(2)}, u32[]{:S(2)}) collective-permute-start(bf16[8,4,4,16,128]{4,3,2,1,0:T(8,128)(2,1)S(1)} %bitcast.11), channel_id=1, source_target_pairs={{64,0},{128,64},{192,128},{65,1},{129,65},{193,129},{66,2},{130,66... | collective-permute-start | bytes 1572872 | tf_op jit(solution)/shard_map/ppermute | solution.py:216
  48.5 0.0 copy-done
  48.5 0.0 copy-done.2
  48.5 2.8 %shard_map.65 = (bf16[64,4,2,16,128]{4,3,2,1,0:T(8,128)(2,1)S(1)}, bf16[4,256,256]{2,1,0:T(8,128)(2,1)S(1)}) custom-call(bf16[16,4,4,16,128]{4,3,2,1,0:T(8,128)(2,1)S(1)} %bitcast.8, bf16[512,512]{1,0:T(8,128)(2,1)S(1)} %copy-done, bf16[128,128]{1,0:T(8,128)(2,1)S(1)} %copy-done.2), custom_call_target="tpu_custom_call" | custom-call | tf_op jit(solution)/shard_map/pallas_call | solution.py:218
  51.3 6.6 %collective-permute-done.halo_ref = bf16[8,4,4,16,128]{4,3,2,1,0:T(8,128)(2,1)S(1)} collective-permute-done((bf16[8,4,4,16,128]{4,3,2,1,0:T(8,128)(2,1)S(1)}, bf16[8,4,4,16,128]{4,3,2,1,0:T(8,128)(2,1)S(1)}, u32[]{:S(2)}, u32[]{:S(2)}) %collective-permute-start) | collective-permute-done | bytes 524320 | tf_op jit(solution)/shard_map/ppermute | solution.py:216
  57.9 3.1 %shard_map.66 = bf16[64,4,2,16,128]{4,3,2,1,0:T(8,128)(2,1)S(1)} custom-call(bf16[8,4,4,16,128]{4,3,2,1,0:T(8,128)(2,1)S(1)} %collective-permute-done.halo_ref, bf16[4,256,256]{2,1,0:T(8,128)(2,1)S(1)} %get-tuple-element.7.rest_ref, bf16[512,512]{1,0:T(8,128)(2,1)S(1)} %copy-done, bf16[128,128]{1,0:T(8,128)(2,1)S(1)} %copy-done.2, ...), custom_call_target="tpu_custom_call", output_to_operand_aliasing={{}: (4, {})} | custom-call | tf_op jit(solution)/shard_map/pallas_call | solution.py:224
  61.0 0.0 copy-start.1
  61.0 51.0 %all_to_all.11 = bf16[64,128,128]{2,1,0:T(8,128)(2,1)S(1)} all-to-all(bf16[64,128,128]{2,1,0:T(8,128)(2,1)S(1)} %bitcast.7), channel_id=1, replica_groups=mesh['row'=4,'col'=16,'tm'=4] {'col','tm'}, dimensions={0} | all-to-all | bytes 4194304 | tf_op jit(solution)/shard_map/all_to_all | solution.py:237
  112.0 0.0 copy-done.1
  112.0 2.4 %shard_map.67 = bf16[8,256,256]{2,1,0:T(8,128)(2,1)} custom-call(bf16[8192,128]{1,0:T(8,128)(2,1)S(1)} %bitcast.6, bf16[512,256]{1,0:T(8,128)(2,1)S(1)} %copy-done.1), custom_call_target="tpu_custom_call" | custom-call | tf_op jit(solution)/shard_map/pallas_call | solution.py:239
  (1 shorter events, 0.0 us)
Async XLA Ops:
  3.8 44.7 %copy-start = (bf16[512,512]{1,0:T(8,128)(2,1)S(1)}, bf16[512,512]{1,0:T(8,128)(2,1)}, u32[]{:S(2)}) copy-start(bf16[512,512]{1,0:T(8,128)(2,1)} %constant.9.clone.swap_ref) | copy-start | bytes 1572868
  3.8 44.7 %copy-start.2 = (bf16[128,128]{1,0:T(8,128)(2,1)S(1)}, bf16[128,128]{1,0:T(8,128)(2,1)}, u32[]{:S(2)}) copy-start(bf16[128,128]{1,0:T(8,128)(2,1)} %constant.10.clone.flip_ref) | copy-start | bytes 98308
  44.2 13.7 %collective-permute-start = (bf16[8,4,4,16,128]{4,3,2,1,0:T(8,128)(2,1)S(1)}, bf16[8,4,4,16,128]{4,3,2,1,0:T(8,128)(2,1)S(1)}, u32[]{:S(2)}, u32[]{:S(2)}) collective-permute-start(bf16[8,4,4,16,128]{4,3,2,1,0:T(8,128)(2,1)S(1)} %bitcast.11), channel_id=1, source_target_pairs={{64,0},{128,64},{192,128},{65,1},{129,65},{193,129},{66,2},{130,66... | collective-permute-start | bytes 1572872 | tf_op jit(solution)/shard_map/ppermute | solution.py:216
  61.0 51.0 %copy-start.1 = (bf16[512,256]{1,0:T(8,128)(2,1)S(1)}, bf16[512,256]{1,0:T(8,128)(2,1)}, u32[]{:S(2)}) copy-start(bf16[512,256]{1,0:T(8,128)(2,1)} %constant.11.clone.table_ref) | copy-start | bytes 786436

commit v4 on v2

--- a/solution.py
+++ b/solution.py
@@ -48,14 +48,14 @@
     return lax.dot_general(left, right, (((1,), (1,)), ((), ())), preferred_element_type=jnp.float32)
 
 
-def whiten_kernel(flags_ref, traces_ref, table_ref, out_ref, scratch):
+def whiten_kernel(flags_ref, traces_ref, table_ref, out_ref, scratch, rounded, sems):
     band = zero_one((HALF, 2 * HALF), lambda r, c: jnp.abs(r - c % HALF) <= SMOOTH)
     bin_index = lax.broadcasted_iota(jnp.int32, (HALF, LANES), 0)
     count = jnp.minimum(bin_index + SMOOTH, HALF - 1) - jnp.maximum(bin_index - SMOOTH, 0) + 1
     inverse = 1.0 / count.astype(jnp.float32)
     lane_block = lax.broadcasted_iota(jnp.int32, (1, LANES), 1) // 32
     table = table_ref[...]
-    width = 4
+    width = 8
     for start in range(0, 8, width):
         rows = jnp.concatenate(
             [traces_ref[high, start + low] for low in range(width) for high in range(4)], axis=0
@@ -75,15 +75,31 @@
             amplitude = live * lax.rsqrt(total[:, lanes] * inverse + 1e-06)
             scratch[pl.ds(channel_low, HALF, stride=16), :] = real[:, lanes] * amplitude
             scratch[pl.ds(8 + channel_low, HALF, stride=16), :] = imag[:, lanes] * amplitude
-    out_ref[...] = scratch[...].astype(jnp.bfloat16)
-
-
-def cross_kernel(received_ref, out_ref, window):
+    copies = []
+    rows = HALF * 4
+    for piece in range(4):
+        part = pl.ds(piece * rows, rows)
+        rounded[part, :] = scratch[part, :].astype(jnp.bfloat16)
+        copies.append(pltpu.make_async_copy(rounded.at[part], out_ref.at[part], sems.at[piece]))
+        copies[-1].start()
+    for copy in copies:
+        copy.wait()
+
+
+def swap_table():
+    r = np.arange(4 * LANES)[:, None]
+    c = np.arange(4 * LANES)[None, :]
+    same = (r % 32 == c % 32) & (r // 32 % 4 == c // 128) & (r // 128 == c // 32 % 4)
+    return same.astype(np.float32).astype(jnp.bfloat16)
+
+
+def flip_table():
+    return np.eye(LANES, dtype=np.float32)[::-1].astype(jnp.bfloat16)
+
+
+def cross_kernel(received_ref, swap_ref, flip_ref, out_ref, window, own):
     window[CHANNELS:, :] = jnp.zeros((OFFS, 2 * LANES), jnp.bfloat16)
-    swap = zero_one(
-        (4 * LANES, 4 * LANES),
-        lambda r, c: (r % 32 == c % 32) & (r // 32 % 4 == c // 128) & (r // 128 == c // 32 % 4),
-    )
+    swap = swap_ref[...]
     group = 16
     for first in range(0, TILES, group):
         side_by_side = jnp.concatenate(
@@ -97,28 +113,23 @@
                 start = (first + tile) * 32
                 window[start : start + 32, part * LANES : (part + 1) * LANES] = rows.astype(jnp.bfloat16)
 
-    flip = zero_one((LANES, LANES), lambda r, c: r + c == LANES - 1)
-
-    def step(index, carry):
-        start = pl.multiple_of(index * LANES, LANES)
-        own = product(flip, window[pl.ds(start, LANES), :])
-        real, imag = own[:, :LANES], own[:, LANES:]
-        others = window[pl.ds(start, LANES + OFFS), :]
-        rows = jnp.concatenate(
-            [jnp.concatenate([real, imag], axis=1), jnp.concatenate([imag, -real], axis=1)], axis=0
-        ).astype(jnp.bfloat16)
-        both_parts = product_nt(rows, others)
+    flip = flip_ref[...]
+    for block in range(CHANNELS // LANES):
+        turned = product(flip, window[block * LANES : (block + 1) * LANES, :])
+        real, imag = turned[:, :LANES], turned[:, LANES:]
+        own[block, :LANES] = jnp.concatenate([real, imag], axis=1).astype(jnp.bfloat16)
+        own[block, LANES:] = jnp.concatenate([imag, -real], axis=1).astype(jnp.bfloat16)
+
+    for block in range(CHANNELS // LANES):
+        start = block * LANES
+        both_parts = product_nt(own[block], window[start : start + LANES + OFFS, :])
         for part in range(2):
             cross = both_parts[part * LANES : (part + 1) * LANES]
             cross = pltpu.roll(cross, OFFS, 1, stride=1, stride_axis=0)
             for place in range(16):
                 eight = cross[8 * place : 8 * place + 8]
                 halves = jnp.concatenate([eight[:, :LANES], eight[:, LANES : 2 * LANES]], axis=0)
-                out_ref[index * 16 + 15 - place, part] = halves.astype(jnp.bfloat16)
-        return carry
-
-    steps = CHANNELS // LANES
-    lax.fori_loop(0, steps, step, 0, unroll=steps)
+                out_ref[block * 16 + 15 - place, part] = halves.astype(jnp.bfloat16)
 
 
 def lag_kernel(received_ref, table_ref, out_ref, lags, sems):
@@ -135,9 +146,10 @@
         lags[channel] = lax.dot_general(
             both, table, (((0,), (0,)), ((), ())), preferred_element_type=jnp.float32
         ).astype(jnp.bfloat16)
-        copy = pltpu.make_async_copy(lags.at[channel], out_ref.at[channel], sems.at[channel])
-        copy.start()
-        copies.append(copy)
+        if channel % 2:
+            pair = pl.ds(channel - 1, 2)
+            copies.append(pltpu.make_async_copy(lags.at[pair], out_ref.at[pair], sems.at[channel // 2]))
+            copies[-1].start()
     for copy in copies:
         copy.wait()
 
@@ -157,24 +169,32 @@
     whitened = call(
         whiten_kernel,
         (HALF * 16, LANES),
-        [pltpu.VMEM((HALF * 16, LANES), jnp.float32)],
+        [
+            pltpu.VMEM((HALF * 16, LANES), jnp.float32),
+            pltpu.VMEM((HALF * 16, LANES), jnp.bfloat16),
+            pltpu.SemaphoreType.DMA((4,)),
+        ],
         63,
         in_specs=[pl.BlockSpec(memory_space=pltpu.SMEM), vmem, vmem],
+        out_specs=pl.BlockSpec(memory_space=pltpu.HBM),
     )(live_flags, traces.reshape(4, 8, 32, NFFT), jnp.asarray(dft_table_t()))
     one_bin = lax.all_to_all(whitened.reshape(HALF, 16, LANES), AXES, 0, 0, tiled=True)
 
     cross = call(
         cross_kernel,
         (HALF, 2, 16, LANES),
-        [pltpu.VMEM((CHANNELS + OFFS, 2 * LANES), jnp.bfloat16)],
+        [
+            pltpu.VMEM((CHANNELS + OFFS, 2 * LANES), jnp.bfloat16),
+            pltpu.VMEM((CHANNELS // LANES, 2 * LANES, 2 * LANES), jnp.bfloat16),
+        ],
         40,
-    )(one_bin.reshape(TILES, 4, 16, LANES))
+    )(one_bin.reshape(TILES, 4, 16, LANES), jnp.asarray(swap_table()), jnp.asarray(flip_table()))
     all_bins = lax.all_to_all(cross.reshape(HALF, 32, LANES), AXES, 0, 0, tiled=True)
 
     return call(
         lag_kernel,
         (8, OFFS, LAGS),
-        [pltpu.VMEM((8, OFFS, LAGS), jnp.bfloat16), pltpu.SemaphoreType.DMA((8,))],
+        [pltpu.VMEM((8, OFFS, LAGS), jnp.bfloat16), pltpu.SemaphoreType.DMA((4,))],
         40,
         in_specs=[vmem, vmem],
         out_specs=pl.BlockSpec(memory_space=pltpu.HBM),

time: 117 us -> 114 us (0.974)
  Pallas kernels: 11.8 us -> 8.44 us
    pallas_call x1, Pallas kernels: 4.2 us -> 2.19 us  [body(): call(cross_kernel, (HALF, 2, 16, LANES), [pltpu.VMEM((CHANNELS + OFFS, 2...]
where the time goes in v4:
time: 114 us
  blocking collectives  105 us (92%)
  Pallas kernels  8.44 us (7%)
    all_to_all x1, blocking collectives, body(): lax.all_to_all(cross.reshape(HALF, 32, LANES), AXES, 0, 0, tiled=True)  59.4 us
    all_to_all x1, blocking collectives, body(): lax.all_to_all(whitened.reshape(HALF, 16, LANES), AXES, 0, 0, tiled=True)  46 us
    pallas_call x1, Pallas kernels, body(): call(whiten_kernel, (HALF * 16, LANES), [pltpu.VMEM((HALF * 16, LANES), j...  3.87 us
    pallas_call x1, Pallas kernels, body(): call(lag_kernel, (8, OFFS, LAGS), [pltpu.VMEM((8, OFFS, LAGS), jnp.bfloat...  2.38 us

profile of v4, /device:TPU:1, one launch (start us, length us, event | category | flops | bytes accessed | tf_op | source)
XLA Modules:
  0.0 113.8 jit_solution(2419530391536549743)
XLA Ops:
  0.0 0.0 copy-start
  0.0 0.0 copy-start.2
  0.0 3.9 %shard_map.64 = bf16[4096,128]{1,0:T(8,128)(2,1)} custom-call(s32[32]{0:T(128)} %flags_ref.1, bf16[4,8,32,512]{3,2,1,0:T(8,128)(2,1)} %bitcast.9, bf16[512,512]{1,0:T(8,128)(2,1)} %constant.8.clone.table_ref), custom_call_target="tpu_custom_call" | custom-call | tf_op jit(solution)/shard_map/pallas_call | solution.py:169
  3.9 46.0 %all_to_all.10 = bf16[256,16,128]{2,1,0:T(8,128)(2,1)S(1)} all-to-all(bf16[256,16,128]{2,1,0:T(8,128)(2,1)} %bitcast.8), channel_id=1, replica_groups=mesh['row'=4,'col'=16,'tm'=4] {'row','col','tm'}, dimensions={0} | all-to-all | bytes 2097152 | tf_op jit(solution)/shard_map/all_to_all | solution.py:181
  49.9 0.0 copy-done
  49.9 0.0 copy-done.2
  49.9 2.2 %shard_map.65 = bf16[256,2,16,128]{3,2,1,0:T(8,128)(2,1)S(1)} custom-call(bf16[64,4,16,128]{3,2,1,0:T(8,128)(2,1)S(1)} %bitcast.7, bf16[512,512]{1,0:T(8,128)(2,1)S(1)} %copy-done, bf16[128,128]{1,0:T(8,128)(2,1)S(1)} %copy-done.2), custom_call_target="tpu_custom_call" | custom-call | tf_op jit(solution)/shard_map/pallas_call | solution.py:183
  52.1 0.0 copy-start.1
  52.1 59.4 %all_to_all.11 = bf16[256,32,128]{2,1,0:T(8,128)(2,1)S(1)} all-to-all(bf16[256,32,128]{2,1,0:T(8,128)(2,1)S(1)} %bitcast.5), channel_id=1, replica_groups=mesh['row'=4,'col'=16,'tm'=4] {'row','col','tm'}, dimensions={0} | all-to-all | bytes 4194304 | tf_op jit(solution)/shard_map/all_to_all | solution.py:192
  111.4 0.0 copy-done.1
  111.4 2.4 %shard_map.66 = bf16[8,256,256]{2,1,0:T(8,128)(2,1)} custom-call(bf16[8192,128]{1,0:T(8,128)(2,1)S(1)} %bitcast.6, bf16[512,256]{1,0:T(8,128)(2,1)S(1)} %copy-done.1), custom_call_target="tpu_custom_call" | custom-call | tf_op jit(solution)/shard_map/pallas_call | solution.py:194
Async XLA Ops:
  0.0 49.9 %copy-start = (bf16[512,512]{1,0:T(8,128)(2,1)S(1)}, bf16[512,512]{1,0:T(8,128)(2,1)}, u32[]{:S(2)}) copy-start(bf16[512,512]{1,0:T(8,128)(2,1)} %constant.9.clone.swap_ref) | copy-start | bytes 1572868
  0.0 49.9 %copy-start.2 = (bf16[128,128]{1,0:T(8,128)(2,1)S(1)}, bf16[128,128]{1,0:T(8,128)(2,1)}, u32[]{:S(2)}) copy-start(bf16[128,128]{1,0:T(8,128)(2,1)} %constant.10.clone.flip_ref) | copy-start | bytes 98308
  52.1 59.4 %copy-start.1 = (bf16[512,256]{1,0:T(8,128)(2,1)S(1)}, bf16[512,256]{1,0:T(8,128)(2,1)}, u32[]{:S(2)}) copy-start(bf16[512,256]{1,0:T(8,128)(2,1)} %constant.11.clone.table_ref) | copy-start | bytes 786436

commit v5 on v3

--- a/solution.py
+++ b/solution.py
@@ -7,6 +7,7 @@
 from jax.sharding import PartitionSpec as P
 
 NFFT = 512
+LANES = 128
 HALF = 256
 OFFS = 256
 LAGS = 256
@@ -16,7 +17,7 @@
 GROUP = 64
 BINS = HALF // GROUP
 ROW = 512
-LANES = 128
+HALF_BLOCKS = ROW // 2 // LANES
 MIB = 1024 * 1024
 
 
@@ -113,46 +114,52 @@
             window[index, start : start + 32, part * LANES : (part + 1) * LANES] = rows.astype(jnp.bfloat16)
 
 
-def cross_block(window, index, start, flip, out_ref, first_place):
-    own = product(flip, window[index, start : start + LANES, :])
-    real, imag = own[:, :LANES], own[:, LANES:]
-    others = window[index, start : start + LANES + OFFS, :]
-    rows = jnp.concatenate(
-        [jnp.concatenate([real, imag], axis=1), jnp.concatenate([imag, -real], axis=1)], axis=0
-    ).astype(jnp.bfloat16)
-    both_parts = product_nt(rows, others)
+def turn_blocks(window, flip, index, own):
+    for block in range(own.shape[1]):
+        turned = product(flip, window[index, block * LANES : (block + 1) * LANES, :])
+        real, imag = turned[:, :LANES], turned[:, LANES:]
+        own[index, block, :LANES] = jnp.concatenate([real, imag], axis=1).astype(jnp.bfloat16)
+        own[index, block, LANES:] = jnp.concatenate([imag, -real], axis=1).astype(jnp.bfloat16)
+
+
+def cross_block(own, others, index, block, out_ref):
+    both_parts = product_nt(own, others)
     for part in range(2):
         cross = both_parts[part * LANES : (part + 1) * LANES]
         cross = pltpu.roll(cross, OFFS, 1, stride=1, stride_axis=0)
         for place in range(16):
             eight = cross[8 * place : 8 * place + 8]
             halves = jnp.concatenate([eight[:, :LANES], eight[:, LANES : 2 * LANES]], axis=0)
-            out_ref[first_place + 15 - place, index, part] = halves.astype(jnp.bfloat16)
-
-
-def near_kernel(received_ref, swap_ref, flip_ref, out_ref, rest_ref, window):
+            out_ref[block * 16 + 15 - place, index, part] = halves.astype(jnp.bfloat16)
+
+
+def near_kernel(received_ref, swap_ref, flip_ref, out_ref, window, own):
     swap = swap_ref[...]
     flip = flip_ref[...]
-    half = window.shape[1] // 2
     for index in range(BINS):
         place_tiles(received_ref, swap, index, window, 0)
-        rest_ref[index] = window[index, half:]
-        for start in range(0, half, LANES):
-            cross_block(window, index, start, flip, out_ref, start // 8)
-
-
-def far_kernel(halo_ref, rest_ref, swap_ref, flip_ref, cross_ref, out_ref, window, results, sems):
+    for index in range(BINS):
+        turn_blocks(window, flip, index, own)
+    for index in range(BINS):
+        for block in range(HALF_BLOCKS):
+            start = block * LANES
+            cross_block(own[index, block], window[index, start : start + LANES + OFFS], index, block, out_ref)
+
+
+def far_kernel(halo_ref, window_ref, own_ref, swap_ref, cross_ref, out_ref, beyond, results, sems):
     del cross_ref
     swap = swap_ref[...]
-    flip = flip_ref[...]
-    half = rest_ref.shape[1]
-    places = half // 8
+    places = ROW // 2 // 8
+    for index in range(BINS):
+        place_tiles(halo_ref, swap, index, beyond, 0)
     copies = []
     for index in range(BINS):
-        window[index, :half] = rest_ref[index]
-        place_tiles(halo_ref, swap, index, window, half)
-        for start in range(0, half, LANES):
-            cross_block(window, index, start, flip, results, start // 8)
+        for block in range(HALF_BLOCKS):
+            start = block * LANES
+            others = jnp.concatenate(
+                [window_ref[index, ROW // 2 + start :], beyond[index, : start + LANES]], axis=0
+            )
+            cross_block(own_ref[index, HALF_BLOCKS + block], others, index, block, results)
         copies.append(
             pltpu.make_async_copy(results.at[:, index], out_ref.at[pl.ds(places, places), index], sems.at[index])
         )
@@ -215,17 +222,21 @@
     first = some_bins[: OFFS // 32]
     halo = lax.ppermute(first, "row", [(1, 0), (2, 1), (3, 2)])
     swap, flip = jnp.asarray(swap_table()), jnp.asarray(flip_table())
-    cross, rest = call(
+    cross, window, own = call(
         near_kernel,
-        [(GROUP, BINS, 2, 16, LANES), (BINS, ROW // 2, 2 * LANES)],
-        [pltpu.VMEM((BINS, ROW, 2 * LANES), jnp.bfloat16)],
+        [
+            (GROUP, BINS, 2, 16, LANES),
+            (BINS, ROW, 2 * LANES),
+            (BINS, 2 * HALF_BLOCKS, 2 * LANES, 2 * LANES),
+        ],
+        [],
         32,
     )(some_bins, swap, flip)
     cross = call(
         far_kernel,
         (GROUP, BINS, 2, 16, LANES),
         [
-            pltpu.VMEM((BINS, ROW // 2 + OFFS, 2 * LANES), jnp.bfloat16),
+            pltpu.VMEM((BINS, OFFS, 2 * LANES), jnp.bfloat16),
             pltpu.VMEM((GROUP // 2, BINS, 2, 16, LANES), jnp.bfloat16),
             pltpu.SemaphoreType.DMA((BINS,)),
         ],
@@ -233,7 +244,7 @@
         in_specs=[vmem, vmem, vmem, vmem, anywhere],
         out_specs=anywhere,
         input_output_aliases={4: 0},
-    )(halo, rest, swap, flip, cross)
+    )(halo, window, own, swap, cross)
     all_bins = lax.all_to_all(cross.reshape(GROUP, BINS * 32, LANES), GROUP_AXES, 0, 0, tiled=True)
 
     return call(

time: 115 us -> 113 us (0.983)
  Pallas kernels: 12.1 us -> 9.94 us
    pallas_call x2, Pallas kernels: 5.88 us -> 3.75 us  [the longest x1 2.1 us: body(): call(far_kernel, (GROUP, BINS, 2, 16, LANES), [pltpu.VMEM((BINS, OFFS, 2...]
  transfers between devices with their start and end apart: 1 -> 1, of which waited for: 1 -> 1; matrix products, arithmetic and copies ran while one was open for 0% -> 0% of each run, Pallas kernels for 2% -> 1%
where the time goes in v5:
time: 113 us
  blocking collectives  91 us (81%)
  Pallas kernels  9.94 us (9%)
  waiting for transfers between devices  7.68 us (7%)
  starting transfers between devices  4.33 us (4%)
    all_to_all x1, blocking collectives, body(): lax.all_to_all(cross.reshape(GROUP, BINS * 32, LANES), GROUP_AXES, 0, 0,...  50.7 us
    all_to_all x1, blocking collectives, body(): lax.all_to_all(whitened.reshape(GROUP, BINS, 16, LANES), GROUP_AXES, 0, 0...  40.3 us
    ppermute x1, waiting for transfers between devices, body(): halo = lax.ppermute(first, 'row', [(1, 0), (2, 1), (3, 2)])  7.68 us
    ppermute x1, starting transfers between devices, body(): halo = lax.ppermute(first, 'row', [(1, 0), (2, 1), (3, 2)])  4.33 us
    pallas_call x1, Pallas kernels, body(): call(whiten_kernel, (HALF * 16, LANES), [pltpu.VMEM((HALF * 16, LANES), j...  3.81 us
    pallas_call x1, Pallas kernels, body(): call(lag_kernel, (8, OFFS, LAGS), [pltpu.VMEM((8, OFFS, LAGS), jnp.bfloat...  2.38 us
  transfers between devices with their start and end apart: 1, of which 1 were waited for; matrix products, arithmetic and copies ran while one was open for 0% of the time, Pallas kernels for 1%

profile of v5, /device:TPU:1, one launch (start us, length us, event | category | flops | bytes accessed | tf_op | source)
XLA Modules:
  0.0 113.1 jit_solution(13007709548159068586)
XLA Ops:
  0.0 3.8 %shard_map.64 = bf16[4096,128]{1,0:T(8,128)(2,1)} custom-call(s32[32]{0:T(128)} %flags_ref.1, bf16[4,8,32,512]{3,2,1,0:T(8,128)(2,1)} %bitcast.10, bf16[512,512]{1,0:T(8,128)(2,1)} %constant.8.clone.table_ref), custom_call_target="tpu_custom_call" | custom-call | tf_op jit(solution)/shard_map/pallas_call | solution.py:207
  3.8 0.0 copy-start
  3.8 0.0 copy-start.2
  3.8 40.3 %all_to_all.10 = bf16[64,4,16,128]{3,2,1,0:T(8,128)(2,1)S(1)} all-to-all(bf16[64,4,16,128]{3,2,1,0:T(8,128)(2,1)} %bitcast.9), channel_id=1, replica_groups=mesh['row'=4,'col'=16,'tm'=4] {'col','tm'}, dimensions={0} | all-to-all | bytes 2097152 | tf_op jit(solution)/shard_map/all_to_all | solution.py:219
  44.2 4.3 %collective-permute-start = (bf16[8,4,4,16,128]{4,3,2,1,0:T(8,128)(2,1)S(1)}, bf16[8,4,4,16,128]{4,3,2,1,0:T(8,128)(2,1)S(1)}, u32[]{:S(2)}, u32[]{:S(2)}) collective-permute-start(bf16[8,4,4,16,128]{4,3,2,1,0:T(8,128)(2,1)S(1)} %bitcast.11), channel_id=1, source_target_pairs={{64,0},{128,64},{192,128},{65,1},{129,65},{193,129},{66,2},{130,66... | collective-permute-start | bytes 1572872 | tf_op jit(solution)/shard_map/ppermute | solution.py:223
  48.5 0.0 copy-done
  48.5 0.0 copy-done.2
  48.5 1.6 %shard_map.65 = (bf16[64,4,2,16,128]{4,3,2,1,0:T(8,128)(2,1)S(1)}, bf16[4,512,256]{2,1,0:T(8,128)(2,1)S(1)}, bf16[4,4,256,256]{3,2,1,0:T(8,128)(2,1)S(1)}) custom-call(bf16[16,4,4,16,128]{4,3,2,1,0:T(8,128)(2,1)S(1)} %bitcast.8, bf16[512,512]{1,0:T(8,128)(2,1)S(1)} %copy-done, bf16[128,128]{1,0:T(8,128)(2,1)S(1)} %copy-done.2), custom_call_target="tpu_custom_call" | custom-call | tf_op jit(solution)/shard_map/pallas_call | solution.py:225
  50.2 7.7 %collective-permute-done.halo_ref = bf16[8,4,4,16,128]{4,3,2,1,0:T(8,128)(2,1)S(1)} collective-permute-done((bf16[8,4,4,16,128]{4,3,2,1,0:T(8,128)(2,1)S(1)}, bf16[8,4,4,16,128]{4,3,2,1,0:T(8,128)(2,1)S(1)}, u32[]{:S(2)}, u32[]{:S(2)}) %collective-permute-start) | collective-permute-done | bytes 524320 | tf_op jit(solution)/shard_map/ppermute | solution.py:223
  57.9 2.1 %shard_map.66 = bf16[64,4,2,16,128]{4,3,2,1,0:T(8,128)(2,1)S(1)} custom-call(bf16[8,4,4,16,128]{4,3,2,1,0:T(8,128)(2,1)S(1)} %collective-permute-done.halo_ref, bf16[4,512,256]{2,1,0:T(8,128)(2,1)S(1)} %get-tuple-element.8.window_ref, bf16[4,4,256,256]{3,2,1,0:T(8,128)(2,1)S(1)} %get-tuple-element.9.own_ref, ...), custom_call_target="tpu_custom_call", output_to_operand_aliasing={{}: (4, {})} | custom-call | tf_op jit(solution)/shard_map/pallas_call | solution.py:235
  60.0 0.0 copy-start.1
  60.0 50.7 %all_to_all.11 = bf16[64,128,128]{2,1,0:T(8,128)(2,1)S(1)} all-to-all(bf16[64,128,128]{2,1,0:T(8,128)(2,1)S(1)} %bitcast.7), channel_id=1, replica_groups=mesh['row'=4,'col'=16,'tm'=4] {'col','tm'}, dimensions={0} | all-to-all | bytes 4194304 | tf_op jit(solution)/shard_map/all_to_all | solution.py:248
  110.7 0.0 copy-done.1
  110.7 2.4 %shard_map.67 = bf16[8,256,256]{2,1,0:T(8,128)(2,1)} custom-call(bf16[8192,128]{1,0:T(8,128)(2,1)S(1)} %bitcast.6, bf16[512,256]{1,0:T(8,128)(2,1)S(1)} %copy-done.1), custom_call_target="tpu_custom_call" | custom-call | tf_op jit(solution)/shard_map/pallas_call | solution.py:250
  (1 shorter events, 0.0 us)
Async XLA Ops:
  3.8 44.7 %copy-start = (bf16[512,512]{1,0:T(8,128)(2,1)S(1)}, bf16[512,512]{1,0:T(8,128)(2,1)}, u32[]{:S(2)}) copy-start(bf16[512,512]{1,0:T(8,128)(2,1)} %constant.9.clone.swap_ref) | copy-start | bytes 1572868
  3.8 44.7 %copy-start.2 = (bf16[128,128]{1,0:T(8,128)(2,1)S(1)}, bf16[128,128]{1,0:T(8,128)(2,1)}, u32[]{:S(2)}) copy-start(bf16[128,128]{1,0:T(8,128)(2,1)} %constant.10.clone.flip_ref) | copy-start | bytes 98308
  44.2 13.7 %collective-permute-start = (bf16[8,4,4,16,128]{4,3,2,1,0:T(8,128)(2,1)S(1)}, bf16[8,4,4,16,128]{4,3,2,1,0:T(8,128)(2,1)S(1)}, u32[]{:S(2)}, u32[]{:S(2)}) collective-permute-start(bf16[8,4,4,16,128]{4,3,2,1,0:T(8,128)(2,1)S(1)} %bitcast.11), channel_id=1, source_target_pairs={{64,0},{128,64},{192,128},{65,1},{129,65},{193,129},{66,2},{130,66... | collective-permute-start | bytes 1572872 | tf_op jit(solution)/shard_map/ppermute | solution.py:223
  60.0 50.7 %copy-start.1 = (bf16[512,256]{1,0:T(8,128)(2,1)S(1)}, bf16[512,256]{1,0:T(8,128)(2,1)}, u32[]{:S(2)}) copy-start(bf16[512,256]{1,0:T(8,128)(2,1)} %constant.11.clone.table_ref) | copy-start | bytes 786436

commit v6 on v4

--- a/solution.py
+++ b/solution.py
@@ -132,16 +132,17 @@
                 out_ref[block * 16 + 15 - place, part] = halves.astype(jnp.bfloat16)
 
 
-def lag_kernel(received_ref, table_ref, out_ref, lags, sems):
+def lag_kernel(received_ref, table_ref, out_ref, wide, lags, sems):
+    wide[...] = received_ref[...].astype(jnp.float32)
     table = table_ref[...]
     copies = []
     for channel in range(8):
         columns = []
         for upper in range(2):
             first = upper * 8 + 7 - channel
-            real = received_ref[pl.ds(first, HALF, stride=32), :]
-            imag = received_ref[pl.ds(16 + first, HALF, stride=32), :]
-            columns.append(jnp.concatenate([real, imag], axis=0))
+            real = wide[pl.ds(first, HALF, stride=32), :]
+            imag = wide[pl.ds(16 + first, HALF, stride=32), :]
+            columns.append(jnp.concatenate([real, imag], axis=0).astype(jnp.bfloat16))
         both = jnp.concatenate(columns, axis=1)
         lags[channel] = lax.dot_general(
             both, table, (((0,), (0,)), ((), ())), preferred_element_type=jnp.float32
@@ -194,7 +195,11 @@
     return call(
         lag_kernel,
         (8, OFFS, LAGS),
-        [pltpu.VMEM((8, OFFS, LAGS), jnp.bfloat16), pltpu.SemaphoreType.DMA((4,))],
+        [
+            pltpu.VMEM((HALF * 32, LANES), jnp.float32),
+            pltpu.VMEM((8, OFFS, LAGS), jnp.bfloat16),
+            pltpu.SemaphoreType.DMA((4,)),
+        ],
         40,
         in_specs=[vmem, vmem],
         out_specs=pl.BlockSpec(memory_space=pltpu.HBM),

time: 114 us -> 115 us (level)
  Pallas kernels: 8.44 us -> 9.75 us
    pallas_call x1, Pallas kernels: 2.38 us -> 3.7 us  [body(): call(lag_kernel, (8, OFFS, LAGS), [pltpu.VMEM((HALF * 32, LANES), jnp.flo...]
where the time goes in v6:
time: 115 us
  blocking collectives  105 us (91%)
  Pallas kernels  9.75 us (8%)
    all_to_all x1, blocking collectives, body(): lax.all_to_all(cross.reshape(HALF, 32, LANES), AXES, 0, 0, tiled=True)  59.4 us
    all_to_all x1, blocking collectives, body(): lax.all_to_all(whitened.reshape(HALF, 16, LANES), AXES, 0, 0, tiled=True)  46 us
    pallas_call x1, Pallas kernels, body(): call(whiten_kernel, (HALF * 16, LANES), [pltpu.VMEM((HALF * 16, LANES), j...  3.87 us
    pallas_call x1, Pallas kernels, body(): call(lag_kernel, (8, OFFS, LAGS), [pltpu.VMEM((HALF * 32, LANES), jnp.flo...  3.7 us

profile of v6, /device:TPU:1, one launch (start us, length us, event | category | flops | bytes accessed | tf_op | source)
XLA Modules:
  0.0 115.1 jit_solution(14124283115249583709)
XLA Ops:
  0.0 0.0 copy-start
  0.0 0.0 copy-start.2
  0.0 3.9 %shard_map.64 = bf16[4096,128]{1,0:T(8,128)(2,1)} custom-call(s32[32]{0:T(128)} %flags_ref.1, bf16[4,8,32,512]{3,2,1,0:T(8,128)(2,1)} %bitcast.9, bf16[512,512]{1,0:T(8,128)(2,1)} %constant.8.clone.table_ref), custom_call_target="tpu_custom_call" | custom-call | tf_op jit(solution)/shard_map/pallas_call | solution.py:170
  3.9 46.0 %all_to_all.10 = bf16[256,16,128]{2,1,0:T(8,128)(2,1)S(1)} all-to-all(bf16[256,16,128]{2,1,0:T(8,128)(2,1)} %bitcast.8), channel_id=1, replica_groups=mesh['row'=4,'col'=16,'tm'=4] {'row','col','tm'}, dimensions={0} | all-to-all | bytes 2097152 | tf_op jit(solution)/shard_map/all_to_all | solution.py:182
  49.9 0.0 copy-done
  49.9 0.0 copy-done.2
  49.9 2.2 %shard_map.65 = bf16[256,2,16,128]{3,2,1,0:T(8,128)(2,1)S(1)} custom-call(bf16[64,4,16,128]{3,2,1,0:T(8,128)(2,1)S(1)} %bitcast.7, bf16[512,512]{1,0:T(8,128)(2,1)S(1)} %copy-done, bf16[128,128]{1,0:T(8,128)(2,1)S(1)} %copy-done.2), custom_call_target="tpu_custom_call" | custom-call | tf_op jit(solution)/shard_map/pallas_call | solution.py:184
  52.1 0.0 copy-start.1
  52.1 59.4 %all_to_all.11 = bf16[256,32,128]{2,1,0:T(8,128)(2,1)S(1)} all-to-all(bf16[256,32,128]{2,1,0:T(8,128)(2,1)S(1)} %bitcast.5), channel_id=1, replica_groups=mesh['row'=4,'col'=16,'tm'=4] {'row','col','tm'}, dimensions={0} | all-to-all | bytes 4194304 | tf_op jit(solution)/shard_map/all_to_all | solution.py:193
  111.4 0.0 copy-done.1
  111.4 3.7 %shard_map.66 = bf16[8,256,256]{2,1,0:T(8,128)(2,1)} custom-call(bf16[8192,128]{1,0:T(8,128)(2,1)S(1)} %bitcast.6, bf16[512,256]{1,0:T(8,128)(2,1)S(1)} %copy-done.1), custom_call_target="tpu_custom_call" | custom-call | tf_op jit(solution)/shard_map/pallas_call | solution.py:195
Async XLA Ops:
  0.0 49.9 %copy-start = (bf16[512,512]{1,0:T(8,128)(2,1)S(1)}, bf16[512,512]{1,0:T(8,128)(2,1)}, u32[]{:S(2)}) copy-start(bf16[512,512]{1,0:T(8,128)(2,1)} %constant.9.clone.swap_ref) | copy-start | bytes 1572868
  0.0 49.9 %copy-start.2 = (bf16[128,128]{1,0:T(8,128)(2,1)S(1)}, bf16[128,128]{1,0:T(8,128)(2,1)}, u32[]{:S(2)}) copy-start(bf16[128,128]{1,0:T(8,128)(2,1)} %constant.10.clone.flip_ref) | copy-start | bytes 98308
  52.1 59.4 %copy-start.1 = (bf16[512,256]{1,0:T(8,128)(2,1)S(1)}, bf16[512,256]{1,0:T(8,128)(2,1)}, u32[]{:S(2)}) copy-start(bf16[512,256]{1,0:T(8,128)(2,1)} %constant.11.clone.table_ref) | copy-start | bytes 786436

commit v7 on v5

--- a/solution.py
+++ b/solution.py
@@ -146,26 +146,18 @@
             cross_block(own[index, block], window[index, start : start + LANES + OFFS], index, block, out_ref)
 
 
-def far_kernel(halo_ref, window_ref, own_ref, swap_ref, cross_ref, out_ref, beyond, results, sems):
-    del cross_ref
+def far_kernel(halo_ref, window_ref, own_ref, swap_ref, near_ref, out_ref, beyond):
     swap = swap_ref[...]
-    places = ROW // 2 // 8
     for index in range(BINS):
         place_tiles(halo_ref, swap, index, beyond, 0)
-    copies = []
-    for index in range(BINS):
-        for block in range(HALF_BLOCKS):
+    out_ref[: ROW // 2 // 8] = near_ref[...]
+    for index in range(BINS):
+        for block in range(HALF_BLOCKS, 2 * HALF_BLOCKS):
             start = block * LANES
             others = jnp.concatenate(
-                [window_ref[index, ROW // 2 + start :], beyond[index, : start + LANES]], axis=0
+                [window_ref[index, start:], beyond[index, : start + LANES + OFFS - ROW]], axis=0
             )
-            cross_block(own_ref[index, HALF_BLOCKS + block], others, index, block, results)
-        copies.append(
-            pltpu.make_async_copy(results.at[:, index], out_ref.at[pl.ds(places, places), index], sems.at[index])
-        )
-        copies[-1].start()
-    for copy in copies:
-        copy.wait()
+            cross_block(own_ref[index, block], others, index, block, out_ref)
 
 
 def lag_kernel(received_ref, table_ref, out_ref, lags, sems):
@@ -203,7 +195,6 @@
 def body(traces, live_flags):
     vmem = pl.BlockSpec(memory_space=pltpu.VMEM)
     hbm = pl.BlockSpec(memory_space=pltpu.HBM)
-    anywhere = pl.BlockSpec(memory_space=pl.ANY)
     whitened = call(
         whiten_kernel,
         (HALF * 16, LANES),
@@ -222,10 +213,10 @@
     first = some_bins[: OFFS // 32]
     halo = lax.ppermute(first, "row", [(1, 0), (2, 1), (3, 2)])
     swap, flip = jnp.asarray(swap_table()), jnp.asarray(flip_table())
-    cross, window, own = call(
+    near, window, own = call(
         near_kernel,
         [
-            (GROUP, BINS, 2, 16, LANES),
+            (GROUP // 2, BINS, 2, 16, LANES),
             (BINS, ROW, 2 * LANES),
             (BINS, 2 * HALF_BLOCKS, 2 * LANES, 2 * LANES),
         ],
@@ -235,16 +226,9 @@
     cross = call(
         far_kernel,
         (GROUP, BINS, 2, 16, LANES),
-        [
-            pltpu.VMEM((BINS, OFFS, 2 * LANES), jnp.bfloat16),
-            pltpu.VMEM((GROUP // 2, BINS, 2, 16, LANES), jnp.bfloat16),
-            pltpu.SemaphoreType.DMA((BINS,)),
-        ],
+        [pltpu.VMEM((BINS, OFFS, 2 * LANES), jnp.bfloat16)],
         32,
-        in_specs=[vmem, vmem, vmem, vmem, anywhere],
-        out_specs=anywhere,
-        input_output_aliases={4: 0},
-    )(halo, window, own, swap, cross)
+    )(halo, window, own, swap, near)
     all_bins = lax.all_to_all(cross.reshape(GROUP, BINS * 32, LANES), GROUP_AXES, 0, 0, tiled=True)
 
     return call(

time: 113 us -> 112 us (level)
  no operation moved by 1% of the time
where the time goes in v7:
time: 112 us
  blocking collectives  91 us (81%)
  Pallas kernels  9.03 us (8%)
  waiting for transfers between devices  7.68 us (7%)
  starting transfers between devices  4.33 us (4%)
    all_to_all x1, blocking collectives, body(): lax.all_to_all(cross.reshape(GROUP, BINS * 32, LANES), GROUP_AXES, 0, 0,...  50.7 us
    all_to_all x1, blocking collectives, body(): lax.all_to_all(whitened.reshape(GROUP, BINS, 16, LANES), GROUP_AXES, 0, 0...  40.3 us
    ppermute x1, waiting for transfers between devices, body(): halo = lax.ppermute(first, 'row', [(1, 0), (2, 1), (3, 2)])  7.68 us
    ppermute x1, starting transfers between devices, body(): halo = lax.ppermute(first, 'row', [(1, 0), (2, 1), (3, 2)])  4.33 us
    pallas_call x1, Pallas kernels, body(): call(whiten_kernel, (HALF * 16, LANES), [pltpu.VMEM((HALF * 16, LANES), j...  3.81 us
    pallas_call x1, Pallas kernels, body(): call(lag_kernel, (8, OFFS, LAGS), [pltpu.VMEM((8, OFFS, LAGS), jnp.bfloat...  2.38 us
  transfers between devices with their start and end apart: 1, of which 1 were waited for; matrix products, arithmetic and copies ran while one was open for 0% of the time, Pallas kernels for 1%

profile of v7, /device:TPU:1, one launch (start us, length us, event | category | flops | bytes accessed | tf_op | source)
XLA Modules:
  0.0 112.2 jit_solution(5186964254975072603)
XLA Ops:
  0.0 3.8 %shard_map.64 = bf16[4096,128]{1,0:T(8,128)(2,1)} custom-call(s32[32]{0:T(128)} %flags_ref.1, bf16[4,8,32,512]{3,2,1,0:T(8,128)(2,1)} %bitcast.10, bf16[512,512]{1,0:T(8,128)(2,1)} %constant.8.clone.table_ref), custom_call_target="tpu_custom_call" | custom-call | tf_op jit(solution)/shard_map/pallas_call | solution.py:198
  3.8 0.0 copy-start
  3.8 0.0 copy-start.2
  3.8 40.3 %all_to_all.10 = bf16[64,4,16,128]{3,2,1,0:T(8,128)(2,1)S(1)} all-to-all(bf16[64,4,16,128]{3,2,1,0:T(8,128)(2,1)} %bitcast.9), channel_id=1, replica_groups=mesh['row'=4,'col'=16,'tm'=4] {'col','tm'}, dimensions={0} | all-to-all | bytes 2097152 | tf_op jit(solution)/shard_map/all_to_all | solution.py:210
  44.2 4.3 %collective-permute-start = (bf16[8,4,4,16,128]{4,3,2,1,0:T(8,128)(2,1)S(1)}, bf16[8,4,4,16,128]{4,3,2,1,0:T(8,128)(2,1)S(1)}, u32[]{:S(2)}, u32[]{:S(2)}) collective-permute-start(bf16[8,4,4,16,128]{4,3,2,1,0:T(8,128)(2,1)S(1)} %bitcast.11), channel_id=1, source_target_pairs={{64,0},{128,64},{192,128},{65,1},{129,65},{193,129},{66,2},{130,66... | collective-permute-start | bytes 1572872 | tf_op jit(solution)/shard_map/ppermute | solution.py:214
  48.5 0.0 copy-done
  48.5 0.0 copy-done.2
  48.5 1.6 %shard_map.65 = (bf16[32,4,2,16,128]{4,3,2,1,0:T(8,128)(2,1)S(1)}, bf16[4,512,256]{2,1,0:T(8,128)(2,1)S(1)}, bf16[4,4,256,256]{3,2,1,0:T(8,128)(2,1)S(1)}) custom-call(bf16[16,4,4,16,128]{4,3,2,1,0:T(8,128)(2,1)S(1)} %bitcast.8, bf16[512,512]{1,0:T(8,128)(2,1)S(1)} %copy-done, bf16[128,128]{1,0:T(8,128)(2,1)S(1)} %copy-done.2), custom_call_target="tpu_custom_call" | custom-call | tf_op jit(solution)/shard_map/pallas_call | solution.py:216
  50.2 7.7 %collective-permute-done.halo_ref = bf16[8,4,4,16,128]{4,3,2,1,0:T(8,128)(2,1)S(1)} collective-permute-done((bf16[8,4,4,16,128]{4,3,2,1,0:T(8,128)(2,1)S(1)}, bf16[8,4,4,16,128]{4,3,2,1,0:T(8,128)(2,1)S(1)}, u32[]{:S(2)}, u32[]{:S(2)}) %collective-permute-start) | collective-permute-done | bytes 524320 | tf_op jit(solution)/shard_map/ppermute | solution.py:214
  57.9 1.2 %shard_map.66 = bf16[64,4,2,16,128]{4,3,2,1,0:T(8,128)(2,1)S(1)} custom-call(bf16[8,4,4,16,128]{4,3,2,1,0:T(8,128)(2,1)S(1)} %collective-permute-done.halo_ref, bf16[4,512,256]{2,1,0:T(8,128)(2,1)S(1)} %get-tuple-element.8.window_ref, bf16[4,4,256,256]{3,2,1,0:T(8,128)(2,1)S(1)} %get-tuple-element.9.own_ref, bf16[512,512]{1,0:T(8,128)(2,1)S(1)} %copy-done, ...), custom_call_target="tpu_custom_call" | custom-call | tf_op jit(solution)/shard_map/pallas_call | solution.py:226
  59.1 0.0 copy-start.1
  59.1 50.7 %all_to_all.11 = bf16[64,128,128]{2,1,0:T(8,128)(2,1)S(1)} all-to-all(bf16[64,128,128]{2,1,0:T(8,128)(2,1)S(1)} %bitcast.6), channel_id=1, replica_groups=mesh['row'=4,'col'=16,'tm'=4] {'col','tm'}, dimensions={0} | all-to-all | bytes 4194304 | tf_op jit(solution)/shard_map/all_to_all | solution.py:232
  109.8 0.0 copy-done.1
  109.8 2.4 %shard_map.67 = bf16[8,256,256]{2,1,0:T(8,128)(2,1)} custom-call(bf16[8192,128]{1,0:T(8,128)(2,1)S(1)} %bitcast.7, bf16[512,256]{1,0:T(8,128)(2,1)S(1)} %copy-done.1), custom_call_target="tpu_custom_call" | custom-call | tf_op jit(solution)/shard_map/pallas_call | solution.py:234
  (1 shorter events, 0.0 us)
Async XLA Ops:
  3.8 44.7 %copy-start = (bf16[512,512]{1,0:T(8,128)(2,1)S(1)}, bf16[512,512]{1,0:T(8,128)(2,1)}, u32[]{:S(2)}) copy-start(bf16[512,512]{1,0:T(8,128)(2,1)} %constant.9.clone.swap_ref) | copy-start | bytes 1572868
  3.8 44.7 %copy-start.2 = (bf16[128,128]{1,0:T(8,128)(2,1)S(1)}, bf16[128,128]{1,0:T(8,128)(2,1)}, u32[]{:S(2)}) copy-start(bf16[128,128]{1,0:T(8,128)(2,1)} %constant.10.clone.flip_ref) | copy-start | bytes 98308
  44.2 13.7 %collective-permute-start = (bf16[8,4,4,16,128]{4,3,2,1,0:T(8,128)(2,1)S(1)}, bf16[8,4,4,16,128]{4,3,2,1,0:T(8,128)(2,1)S(1)}, u32[]{:S(2)}, u32[]{:S(2)}) collective-permute-start(bf16[8,4,4,16,128]{4,3,2,1,0:T(8,128)(2,1)S(1)} %bitcast.11), channel_id=1, source_target_pairs={{64,0},{128,64},{192,128},{65,1},{129,65},{193,129},{66,2},{130,66... | collective-permute-start | bytes 1572872 | tf_op jit(solution)/shard_map/ppermute | solution.py:214
  59.1 50.7 %copy-start.1 = (bf16[512,256]{1,0:T(8,128)(2,1)S(1)}, bf16[512,256]{1,0:T(8,128)(2,1)}, u32[]{:S(2)}) copy-start(bf16[512,256]{1,0:T(8,128)(2,1)} %constant.11.clone.table_ref) | copy-start | bytes 786436

commit v8 on v7

--- a/solution.py
+++ b/solution.py
@@ -76,13 +76,15 @@
             for high in range(4):
                 live = jnp.where(lane_block == high, flags_ref[high * 8 + channel_low].astype(jnp.float32), live)
             amplitude = live * lax.rsqrt(total[:, lanes] * inverse + 1e-06)
-            scratch[pl.ds(channel_low, HALF, stride=16), :] = real[:, lanes] * amplitude
-            scratch[pl.ds(8 + channel_low, HALF, stride=16), :] = imag[:, lanes] * amplitude
+            scratch[channel_low] = (real[:, lanes] * amplitude).astype(jnp.bfloat16)
+            scratch[8 + channel_low] = (imag[:, lanes] * amplitude).astype(jnp.bfloat16)
     copies = []
     rows = HALF * 4
     for piece in range(4):
         part = pl.ds(piece * rows, rows)
-        rounded[part, :] = scratch[part, :].astype(jnp.bfloat16)
+        for first in range(piece * HALF // 4, (piece + 1) * HALF // 4, 16):
+            block = jnp.swapaxes(scratch[:, first : first + 16, :], 0, 1)
+            rounded[first * 16 : (first + 16) * 16, :] = block.reshape(HALF, LANES)
         copies.append(pltpu.make_async_copy(rounded.at[part], out_ref.at[part], sems.at[piece]))
         copies[-1].start()
     for copy in copies:
@@ -160,16 +162,18 @@
             cross_block(own_ref[index, block], others, index, block, out_ref)
 
 
-def lag_kernel(received_ref, table_ref, out_ref, lags, sems):
+def lag_kernel(received_ref, table_ref, out_ref, by_row, lags, sems):
+    group = 16
+    for first in range(0, HALF, group):
+        block = received_ref[first * 32 : (first + group) * 32, :].reshape(group, 32, LANES)
+        by_row[:, first : first + group, :] = jnp.swapaxes(block, 0, 1)
     table = table_ref[...]
     copies = []
     for channel in range(8):
         columns = []
         for upper in range(2):
             first = upper * 8 + 7 - channel
-            real = received_ref[pl.ds(first, HALF, stride=32), :]
-            imag = received_ref[pl.ds(16 + first, HALF, stride=32), :]
-            columns.append(jnp.concatenate([real, imag], axis=0))
+            columns.append(jnp.concatenate([by_row[first], by_row[16 + first]], axis=0))
         both = jnp.concatenate(columns, axis=1)
         lags[channel] = lax.dot_general(
             both, table, (((0,), (0,)), ((), ())), preferred_element_type=jnp.float32
@@ -199,7 +203,7 @@
         whiten_kernel,
         (HALF * 16, LANES),
         [
-            pltpu.VMEM((HALF * 16, LANES), jnp.float32),
+            pltpu.VMEM((16, HALF, LANES), jnp.bfloat16),
             pltpu.VMEM((HALF * 16, LANES), jnp.bfloat16),
             pltpu.SemaphoreType.DMA((4,)),
         ],
@@ -234,7 +238,11 @@
     return call(
         lag_kernel,
         (8, OFFS, LAGS),
-        [pltpu.VMEM((8, OFFS, LAGS), jnp.bfloat16), pltpu.SemaphoreType.DMA((4,))],
+        [
+            pltpu.VMEM((32, HALF, LANES), jnp.bfloat16),
+            pltpu.VMEM((8, OFFS, LAGS), jnp.bfloat16),
+            pltpu.SemaphoreType.DMA((4,)),
+        ],
         32,
         in_specs=[vmem, vmem],
         out_specs=hbm,

time: 112 us -> 112 us (level)
  no operation moved by 1% of the time
where the time goes in v8:
time: 112 us
  blocking collectives  91 us (81%)
  Pallas kernels  8.52 us (8%)
  waiting for transfers between devices  7.69 us (7%)
  starting transfers between devices  4.33 us (4%)
    all_to_all x1, blocking collectives, body(): lax.all_to_all(cross.reshape(GROUP, BINS * 32, LANES), GROUP_AXES, 0, 0,...  50.7 us
    all_to_all x1, blocking collectives, body(): lax.all_to_all(whitened.reshape(GROUP, BINS, 16, LANES), GROUP_AXES, 0, 0...  40.3 us
    ppermute x1, waiting for transfers between devices, body(): halo = lax.ppermute(first, 'row', [(1, 0), (2, 1), (3, 2)])  7.69 us
    ppermute x1, starting transfers between devices, body(): halo = lax.ppermute(first, 'row', [(1, 0), (2, 1), (3, 2)])  4.33 us
    pallas_call x1, Pallas kernels, body(): call(whiten_kernel, (HALF * 16, LANES), [pltpu.VMEM((16, HALF, LANES), jn...  3.75 us
  transfers between devices with their start and end apart: 1, of which 1 were waited for; matrix products, arithmetic and copies ran while one was open for 0% of the time, Pallas kernels for 1%

profile of v8, /device:TPU:1, one launch (start us, length us, event | category | flops | bytes accessed | tf_op | source)
XLA Modules:
  0.0 111.6 jit_solution(13986381355518506818)
XLA Ops:
  0.0 3.8 %shard_map.64 = bf16[4096,128]{1,0:T(8,128)(2,1)} custom-call(s32[32]{0:T(128)} %flags_ref.1, bf16[4,8,32,512]{3,2,1,0:T(8,128)(2,1)} %bitcast.10, bf16[512,512]{1,0:T(8,128)(2,1)} %constant.8.clone.table_ref), custom_call_target="tpu_custom_call" | custom-call | tf_op jit(solution)/shard_map/pallas_call | solution.py:202
  3.8 0.0 copy-start
  3.8 0.0 copy-start.2
  3.8 40.3 %all_to_all.10 = bf16[64,4,16,128]{3,2,1,0:T(8,128)(2,1)S(1)} all-to-all(bf16[64,4,16,128]{3,2,1,0:T(8,128)(2,1)} %bitcast.9), channel_id=1, replica_groups=mesh['row'=4,'col'=16,'tm'=4] {'col','tm'}, dimensions={0} | all-to-all | bytes 2097152 | tf_op jit(solution)/shard_map/all_to_all | solution.py:214
  44.1 4.3 %collective-permute-start = (bf16[8,4,4,16,128]{4,3,2,1,0:T(8,128)(2,1)S(1)}, bf16[8,4,4,16,128]{4,3,2,1,0:T(8,128)(2,1)S(1)}, u32[]{:S(2)}, u32[]{:S(2)}) collective-permute-start(bf16[8,4,4,16,128]{4,3,2,1,0:T(8,128)(2,1)S(1)} %bitcast.11), channel_id=1, source_target_pairs={{64,0},{128,64},{192,128},{65,1},{129,65},{193,129},{66,2},{130,66... | collective-permute-start | bytes 1572872 | tf_op jit(solution)/shard_map/ppermute | solution.py:218
  48.4 0.0 copy-done
  48.4 0.0 copy-done.2
  48.5 1.6 %shard_map.65 = (bf16[32,4,2,16,128]{4,3,2,1,0:T(8,128)(2,1)S(1)}, bf16[4,512,256]{2,1,0:T(8,128)(2,1)S(1)}, bf16[4,4,256,256]{3,2,1,0:T(8,128)(2,1)S(1)}) custom-call(bf16[16,4,4,16,128]{4,3,2,1,0:T(8,128)(2,1)S(1)} %bitcast.8, bf16[512,512]{1,0:T(8,128)(2,1)S(1)} %copy-done, bf16[128,128]{1,0:T(8,128)(2,1)S(1)} %copy-done.2), custom_call_target="tpu_custom_call" | custom-call | tf_op jit(solution)/shard_map/pallas_call | solution.py:220
  50.1 7.7 %collective-permute-done.halo_ref = bf16[8,4,4,16,128]{4,3,2,1,0:T(8,128)(2,1)S(1)} collective-permute-done((bf16[8,4,4,16,128]{4,3,2,1,0:T(8,128)(2,1)S(1)}, bf16[8,4,4,16,128]{4,3,2,1,0:T(8,128)(2,1)S(1)}, u32[]{:S(2)}, u32[]{:S(2)}) %collective-permute-start) | collective-permute-done | bytes 524320 | tf_op jit(solution)/shard_map/ppermute | solution.py:218
  57.8 1.2 %shard_map.66 = bf16[64,4,2,16,128]{4,3,2,1,0:T(8,128)(2,1)S(1)} custom-call(bf16[8,4,4,16,128]{4,3,2,1,0:T(8,128)(2,1)S(1)} %collective-permute-done.halo_ref, bf16[4,512,256]{2,1,0:T(8,128)(2,1)S(1)} %get-tuple-element.8.window_ref, bf16[4,4,256,256]{3,2,1,0:T(8,128)(2,1)S(1)} %get-tuple-element.9.own_ref, bf16[512,512]{1,0:T(8,128)(2,1)S(1)} %copy-done, ...), custom_call_target="tpu_custom_call" | custom-call | tf_op jit(solution)/shard_map/pallas_call | solution.py:230
  59.0 0.0 copy-start.1
  59.0 50.7 %all_to_all.11 = bf16[64,128,128]{2,1,0:T(8,128)(2,1)S(1)} all-to-all(bf16[64,128,128]{2,1,0:T(8,128)(2,1)S(1)} %bitcast.6), channel_id=1, replica_groups=mesh['row'=4,'col'=16,'tm'=4] {'col','tm'}, dimensions={0} | all-to-all | bytes 4194304 | tf_op jit(solution)/shard_map/all_to_all | solution.py:236
  109.7 0.0 copy-done.1
  109.7 1.9 %shard_map.67 = bf16[8,256,256]{2,1,0:T(8,128)(2,1)} custom-call(bf16[8192,128]{1,0:T(8,128)(2,1)S(1)} %bitcast.7, bf16[512,256]{1,0:T(8,128)(2,1)S(1)} %copy-done.1), custom_call_target="tpu_custom_call" | custom-call | tf_op jit(solution)/shard_map/pallas_call | solution.py:238
  (1 shorter events, 0.0 us)
Async XLA Ops:
  3.8 44.7 %copy-start = (bf16[512,512]{1,0:T(8,128)(2,1)S(1)}, bf16[512,512]{1,0:T(8,128)(2,1)}, u32[]{:S(2)}) copy-start(bf16[512,512]{1,0:T(8,128)(2,1)} %constant.9.clone.swap_ref) | copy-start | bytes 1572868
  3.8 44.7 %copy-start.2 = (bf16[128,128]{1,0:T(8,128)(2,1)S(1)}, bf16[128,128]{1,0:T(8,128)(2,1)}, u32[]{:S(2)}) copy-start(bf16[128,128]{1,0:T(8,128)(2,1)} %constant.10.clone.flip_ref) | copy-start | bytes 98308
  44.1 13.7 %collective-permute-start = (bf16[8,4,4,16,128]{4,3,2,1,0:T(8,128)(2,1)S(1)}, bf16[8,4,4,16,128]{4,3,2,1,0:T(8,128)(2,1)S(1)}, u32[]{:S(2)}, u32[]{:S(2)}) collective-permute-start(bf16[8,4,4,16,128]{4,3,2,1,0:T(8,128)(2,1)S(1)} %bitcast.11), channel_id=1, source_target_pairs={{64,0},{128,64},{192,128},{65,1},{129,65},{193,129},{66,2},{130,66... | collective-permute-start | bytes 1572872 | tf_op jit(solution)/shard_map/ppermute | solution.py:218
  59.0 50.7 %copy-start.1 = (bf16[512,256]{1,0:T(8,128)(2,1)S(1)}, bf16[512,256]{1,0:T(8,128)(2,1)}, u32[]{:S(2)}) copy-start(bf16[512,256]{1,0:T(8,128)(2,1)} %constant.11.clone.table_ref) | copy-start | bytes 786436

commit v9 on v8

--- a/solution.py
+++ b/solution.py
@@ -58,7 +58,7 @@
     inverse = 1.0 / count.astype(jnp.float32)
     lane_block = lax.broadcasted_iota(jnp.int32, (1, LANES), 1) // 32
     table = table_ref[...]
-    width = 8
+    width = 4
     for start in range(0, 8, width):
         rows = jnp.concatenate(
             [traces_ref[high, start + low] for low in range(width) for high in range(4)], axis=0

time: 112 us -> 112 us (level)
  no operation moved by 1% of the time
where the time goes in v9:
time: 112 us
  blocking collectives  91 us (81%)
  Pallas kernels  8.75 us (8%)
  waiting for transfers between devices  7.69 us (7%)
  starting transfers between devices  4.32 us (4%)
    all_to_all x1, blocking collectives, body(): lax.all_to_all(cross.reshape(GROUP, BINS * 32, LANES), GROUP_AXES, 0, 0,...  50.7 us
    all_to_all x1, blocking collectives, body(): lax.all_to_all(whitened.reshape(GROUP, BINS, 16, LANES), GROUP_AXES, 0, 0...  40.3 us
    ppermute x1, waiting for transfers between devices, body(): halo = lax.ppermute(first, 'row', [(1, 0), (2, 1), (3, 2)])  7.69 us
    ppermute x1, starting transfers between devices, body(): halo = lax.ppermute(first, 'row', [(1, 0), (2, 1), (3, 2)])  4.32 us
    pallas_call x1, Pallas kernels, body(): call(whiten_kernel, (HALF * 16, LANES), [pltpu.VMEM((16, HALF, LANES), jn...  3.98 us
  transfers between devices with their start and end apart: 1, of which 1 were waited for; matrix products, arithmetic and copies ran while one was open for 0% of the time, Pallas kernels for 1%

profile of v9, /device:TPU:1, one launch (start us, length us, event | category | flops | bytes accessed | tf_op | source)
XLA Modules:
  0.0 111.9 jit_solution(14067230655482675248)
XLA Ops:
  0.0 4.0 %shard_map.64 = bf16[4096,128]{1,0:T(8,128)(2,1)} custom-call(s32[32]{0:T(128)} %flags_ref.1, bf16[4,8,32,512]{3,2,1,0:T(8,128)(2,1)} %bitcast.10, bf16[512,512]{1,0:T(8,128)(2,1)} %constant.8.clone.table_ref), custom_call_target="tpu_custom_call" | custom-call | tf_op jit(solution)/shard_map/pallas_call | solution.py:202
  4.0 0.0 copy-start
  4.0 0.0 copy-start.2
  4.0 40.3 %all_to_all.10 = bf16[64,4,16,128]{3,2,1,0:T(8,128)(2,1)S(1)} all-to-all(bf16[64,4,16,128]{3,2,1,0:T(8,128)(2,1)} %bitcast.9), channel_id=1, replica_groups=mesh['row'=4,'col'=16,'tm'=4] {'col','tm'}, dimensions={0} | all-to-all | bytes 2097152 | tf_op jit(solution)/shard_map/all_to_all | solution.py:214
  44.3 4.3 %collective-permute-start = (bf16[8,4,4,16,128]{4,3,2,1,0:T(8,128)(2,1)S(1)}, bf16[8,4,4,16,128]{4,3,2,1,0:T(8,128)(2,1)S(1)}, u32[]{:S(2)}, u32[]{:S(2)}) collective-permute-start(bf16[8,4,4,16,128]{4,3,2,1,0:T(8,128)(2,1)S(1)} %bitcast.11), channel_id=1, source_target_pairs={{64,0},{128,64},{192,128},{65,1},{129,65},{193,129},{66,2},{130,66... | collective-permute-start | bytes 1572872 | tf_op jit(solution)/shard_map/ppermute | solution.py:218
  48.7 0.0 copy-done
  48.7 0.0 copy-done.2
  48.7 1.6 %shard_map.65 = (bf16[32,4,2,16,128]{4,3,2,1,0:T(8,128)(2,1)S(1)}, bf16[4,512,256]{2,1,0:T(8,128)(2,1)S(1)}, bf16[4,4,256,256]{3,2,1,0:T(8,128)(2,1)S(1)}) custom-call(bf16[16,4,4,16,128]{4,3,2,1,0:T(8,128)(2,1)S(1)} %bitcast.8, bf16[512,512]{1,0:T(8,128)(2,1)S(1)} %copy-done, bf16[128,128]{1,0:T(8,128)(2,1)S(1)} %copy-done.2), custom_call_target="tpu_custom_call" | custom-call | tf_op jit(solution)/shard_map/pallas_call | solution.py:220
  50.3 7.7 %collective-permute-done.halo_ref = bf16[8,4,4,16,128]{4,3,2,1,0:T(8,128)(2,1)S(1)} collective-permute-done((bf16[8,4,4,16,128]{4,3,2,1,0:T(8,128)(2,1)S(1)}, bf16[8,4,4,16,128]{4,3,2,1,0:T(8,128)(2,1)S(1)}, u32[]{:S(2)}, u32[]{:S(2)}) %collective-permute-start) | collective-permute-done | bytes 524320 | tf_op jit(solution)/shard_map/ppermute | solution.py:218
  58.0 1.2 %shard_map.66 = bf16[64,4,2,16,128]{4,3,2,1,0:T(8,128)(2,1)S(1)} custom-call(bf16[8,4,4,16,128]{4,3,2,1,0:T(8,128)(2,1)S(1)} %collective-permute-done.halo_ref, bf16[4,512,256]{2,1,0:T(8,128)(2,1)S(1)} %get-tuple-element.8.window_ref, bf16[4,4,256,256]{3,2,1,0:T(8,128)(2,1)S(1)} %get-tuple-element.9.own_ref, bf16[512,512]{1,0:T(8,128)(2,1)S(1)} %copy-done, ...), custom_call_target="tpu_custom_call" | custom-call | tf_op jit(solution)/shard_map/pallas_call | solution.py:230
  59.2 0.0 copy-start.1
  59.2 50.7 %all_to_all.11 = bf16[64,128,128]{2,1,0:T(8,128)(2,1)S(1)} all-to-all(bf16[64,128,128]{2,1,0:T(8,128)(2,1)S(1)} %bitcast.6), channel_id=1, replica_groups=mesh['row'=4,'col'=16,'tm'=4] {'col','tm'}, dimensions={0} | all-to-all | bytes 4194304 | tf_op jit(solution)/shard_map/all_to_all | solution.py:236
  109.9 0.0 copy-done.1
  109.9 1.9 %shard_map.67 = bf16[8,256,256]{2,1,0:T(8,128)(2,1)} custom-call(bf16[8192,128]{1,0:T(8,128)(2,1)S(1)} %bitcast.7, bf16[512,256]{1,0:T(8,128)(2,1)S(1)} %copy-done.1), custom_call_target="tpu_custom_call" | custom-call | tf_op jit(solution)/shard_map/pallas_call | solution.py:238
  (1 shorter events, 0.0 us)
Async XLA Ops:
  4.0 44.7 %copy-start = (bf16[512,512]{1,0:T(8,128)(2,1)S(1)}, bf16[512,512]{1,0:T(8,128)(2,1)}, u32[]{:S(2)}) copy-start(bf16[512,512]{1,0:T(8,128)(2,1)} %constant.9.clone.swap_ref) | copy-start | bytes 1572868
  4.0 44.7 %copy-start.2 = (bf16[128,128]{1,0:T(8,128)(2,1)S(1)}, bf16[128,128]{1,0:T(8,128)(2,1)}, u32[]{:S(2)}) copy-start(bf16[128,128]{1,0:T(8,128)(2,1)} %constant.10.clone.flip_ref) | copy-start | bytes 98308
  44.3 13.7 %collective-permute-start = (bf16[8,4,4,16,128]{4,3,2,1,0:T(8,128)(2,1)S(1)}, bf16[8,4,4,16,128]{4,3,2,1,0:T(8,128)(2,1)S(1)}, u32[]{:S(2)}, u32[]{:S(2)}) collective-permute-start(bf16[8,4,4,16,128]{4,3,2,1,0:T(8,128)(2,1)S(1)} %bitcast.11), channel_id=1, source_target_pairs={{64,0},{128,64},{192,128},{65,1},{129,65},{193,129},{66,2},{130,66... | collective-permute-start | bytes 1572872 | tf_op jit(solution)/shard_map/ppermute | solution.py:218
  59.2 50.7 %copy-start.1 = (bf16[512,256]{1,0:T(8,128)(2,1)S(1)}, bf16[512,256]{1,0:T(8,128)(2,1)}, u32[]{:S(2)}) copy-start(bf16[512,256]{1,0:T(8,128)(2,1)} %constant.11.clone.table_ref) | copy-start | bytes 786436

commit v10 on v8

--- a/solution.py
+++ b/solution.py
@@ -17,7 +17,6 @@
 GROUP = 64
 BINS = HALF // GROUP
 ROW = 512
-HALF_BLOCKS = ROW // 2 // LANES
 MIB = 1024 * 1024
 
 
@@ -124,15 +123,21 @@
         own[index, block, LANES:] = jnp.concatenate([imag, -real], axis=1).astype(jnp.bfloat16)
 
 
-def cross_block(own, others, index, block, out_ref):
-    both_parts = product_nt(own, others)
-    for part in range(2):
-        cross = both_parts[part * LANES : (part + 1) * LANES]
-        cross = pltpu.roll(cross, OFFS, 1, stride=1, stride_axis=0)
-        for place in range(16):
-            eight = cross[8 * place : 8 * place + 8]
-            halves = jnp.concatenate([eight[:, :LANES], eight[:, LANES : 2 * LANES]], axis=0)
-            out_ref[block * 16 + 15 - place, index, part] = halves.astype(jnp.bfloat16)
+def skewed(factors, others):
+    both_parts = product_nt(factors, others)
+    shift = both_parts.shape[1] - LANES
+    return [
+        pltpu.roll(both_parts[part * LANES : (part + 1) * LANES], shift, 1, stride=1, stride_axis=0)
+        for part in range(2)
+    ]
+
+
+def store_half(parts, half, out_ref, block, index, upper):
+    lanes = slice(half * LANES, (half + 1) * LANES)
+    for place in range(16):
+        rows = slice(8 * place, 8 * place + 8)
+        both = jnp.concatenate([part[rows, lanes] for part in parts], axis=0)
+        out_ref[block * 16 + 15 - place, index, upper] = both.astype(jnp.bfloat16)
 
 
 def near_kernel(received_ref, swap_ref, flip_ref, out_ref, window, own):
@@ -143,23 +148,27 @@
     for index in range(BINS):
         turn_blocks(window, flip, index, own)
     for index in range(BINS):
-        for block in range(HALF_BLOCKS):
+        for block in range(3):
+            reach = min(3, 4 - block)
             start = block * LANES
-            cross_block(own[index, block], window[index, start : start + LANES + OFFS], index, block, out_ref)
+            parts = skewed(own[index, block], window[index, start : start + reach * LANES])
+            for half in range(reach - 1):
+                store_half(parts, half, out_ref, block, index, half)
 
 
 def far_kernel(halo_ref, window_ref, own_ref, swap_ref, near_ref, out_ref, beyond):
     swap = swap_ref[...]
     for index in range(BINS):
         place_tiles(halo_ref, swap, index, beyond, 0)
-    out_ref[: ROW // 2 // 8] = near_ref[...]
-    for index in range(BINS):
-        for block in range(HALF_BLOCKS, 2 * HALF_BLOCKS):
-            start = block * LANES
-            others = jnp.concatenate(
-                [window_ref[index, start:], beyond[index, : start + LANES + OFFS - ROW]], axis=0
-            )
-            cross_block(own_ref[index, block], others, index, block, out_ref)
+    out_ref[:32] = near_ref[:32]
+    out_ref[32:48, :, 0] = near_ref[32:48, :, 0]
+    for index in range(BINS):
+        tail = window_ref[index, 3 * LANES :]
+        parts = skewed(own_ref[index, 2], jnp.concatenate([tail, beyond[index, :LANES]], axis=0))
+        store_half(parts, 0, out_ref, 2, index, 1)
+        parts = skewed(own_ref[index, 3], jnp.concatenate([tail, beyond[index]], axis=0))
+        for half in range(2):
+            store_half(parts, half, out_ref, 3, index, half)
 
 
 def lag_kernel(received_ref, table_ref, out_ref, by_row, lags, sems):
@@ -172,8 +181,8 @@
     for channel in range(8):
         columns = []
         for upper in range(2):
-            first = upper * 8 + 7 - channel
-            columns.append(jnp.concatenate([by_row[first], by_row[16 + first]], axis=0))
+            first = upper * 16 + 7 - channel
+            columns.append(jnp.concatenate([by_row[first], by_row[8 + first]], axis=0))
         both = jnp.concatenate(columns, axis=1)
         lags[channel] = lax.dot_general(
             both, table, (((0,), (0,)), ((), ())), preferred_element_type=jnp.float32
@@ -220,9 +229,9 @@
     near, window, own = call(
         near_kernel,
         [
-            (GROUP // 2, BINS, 2, 16, LANES),
+            (48, BINS, 2, 16, LANES),
             (BINS, ROW, 2 * LANES),
-            (BINS, 2 * HALF_BLOCKS, 2 * LANES, 2 * LANES),
+            (BINS, ROW // LANES, 2 * LANES, 2 * LANES),
         ],
         [],
         32,

time: 112 us -> 112 us (level)
  transfers between devices with their start and end apart: 1 -> 1, of which waited for: 1 -> 1; matrix products, arithmetic and copies ran while one was open for 0% -> 0% of each run, Pallas kernels for 1% -> 2%
where the time goes in v10:
time: 112 us
  blocking collectives  91 us (81%)
  Pallas kernels  8.66 us (8%)
  waiting for transfers between devices  7.54 us (7%)
  starting transfers between devices  4.33 us (4%)
    all_to_all x1, blocking collectives, body(): lax.all_to_all(cross.reshape(GROUP, BINS * 32, LANES), GROUP_AXES, 0, 0,...  50.7 us
    all_to_all x1, blocking collectives, body(): lax.all_to_all(whitened.reshape(GROUP, BINS, 16, LANES), GROUP_AXES, 0, 0...  40.3 us
    ppermute x1, waiting for transfers between devices, body(): halo = lax.ppermute(first, 'row', [(1, 0), (2, 1), (3, 2)])  7.54 us
    ppermute x1, starting transfers between devices, body(): halo = lax.ppermute(first, 'row', [(1, 0), (2, 1), (3, 2)])  4.33 us
    pallas_call x1, Pallas kernels, body(): call(whiten_kernel, (HALF * 16, LANES), [pltpu.VMEM((16, HALF, LANES), jn...  3.75 us
  transfers between devices with their start and end apart: 1, of which 1 were waited for; matrix products, arithmetic and copies ran while one was open for 0% of the time, Pallas kernels for 2%

profile of v10, /device:TPU:1, one launch (start us, length us, event | category | flops | bytes accessed | tf_op | source)
XLA Modules:
  0.0 111.6 jit_solution(6884263509738268535)
XLA Ops:
  0.0 3.8 %shard_map.64 = bf16[4096,128]{1,0:T(8,128)(2,1)} custom-call(s32[32]{0:T(128)} %flags_ref.1, bf16[4,8,32,512]{3,2,1,0:T(8,128)(2,1)} %bitcast.10, bf16[512,512]{1,0:T(8,128)(2,1)} %constant.8.clone.table_ref), custom_call_target="tpu_custom_call" | custom-call | tf_op jit(solution)/shard_map/pallas_call | solution.py:211
  3.8 0.0 copy-start
  3.8 0.0 copy-start.2
  3.8 40.3 %all_to_all.10 = bf16[64,4,16,128]{3,2,1,0:T(8,128)(2,1)S(1)} all-to-all(bf16[64,4,16,128]{3,2,1,0:T(8,128)(2,1)} %bitcast.9), channel_id=1, replica_groups=mesh['row'=4,'col'=16,'tm'=4] {'col','tm'}, dimensions={0} | all-to-all | bytes 2097152 | tf_op jit(solution)/shard_map/all_to_all | solution.py:223
  44.1 4.3 %collective-permute-start = (bf16[8,4,4,16,128]{4,3,2,1,0:T(8,128)(2,1)S(1)}, bf16[8,4,4,16,128]{4,3,2,1,0:T(8,128)(2,1)S(1)}, u32[]{:S(2)}, u32[]{:S(2)}) collective-permute-start(bf16[8,4,4,16,128]{4,3,2,1,0:T(8,128)(2,1)S(1)} %bitcast.11), channel_id=1, source_target_pairs={{64,0},{128,64},{192,128},{65,1},{129,65},{193,129},{66,2},{130,66... | collective-permute-start | bytes 1572872 | tf_op jit(solution)/shard_map/ppermute | solution.py:227
  48.4 0.0 copy-done
  48.4 0.0 copy-done.2
  48.5 1.8 %shard_map.65 = (bf16[48,4,2,16,128]{4,3,2,1,0:T(8,128)(2,1)S(1)}, bf16[4,512,256]{2,1,0:T(8,128)(2,1)S(1)}, bf16[4,4,256,256]{3,2,1,0:T(8,128)(2,1)S(1)}) custom-call(bf16[16,4,4,16,128]{4,3,2,1,0:T(8,128)(2,1)S(1)} %bitcast.8, bf16[512,512]{1,0:T(8,128)(2,1)S(1)} %copy-done, bf16[128,128]{1,0:T(8,128)(2,1)S(1)} %copy-done.2), custom_call_target="tpu_custom_call" | custom-call | tf_op jit(solution)/shard_map/pallas_call | solution.py:229
  50.3 7.5 %collective-permute-done.halo_ref = bf16[8,4,4,16,128]{4,3,2,1,0:T(8,128)(2,1)S(1)} collective-permute-done((bf16[8,4,4,16,128]{4,3,2,1,0:T(8,128)(2,1)S(1)}, bf16[8,4,4,16,128]{4,3,2,1,0:T(8,128)(2,1)S(1)}, u32[]{:S(2)}, u32[]{:S(2)}) %collective-permute-start) | collective-permute-done | bytes 524320 | tf_op jit(solution)/shard_map/ppermute | solution.py:227
  57.8 1.2 %shard_map.66 = bf16[64,4,2,16,128]{4,3,2,1,0:T(8,128)(2,1)S(1)} custom-call(bf16[8,4,4,16,128]{4,3,2,1,0:T(8,128)(2,1)S(1)} %collective-permute-done.halo_ref, bf16[4,512,256]{2,1,0:T(8,128)(2,1)S(1)} %get-tuple-element.8.window_ref, bf16[4,4,256,256]{3,2,1,0:T(8,128)(2,1)S(1)} %get-tuple-element.9.own_ref, bf16[512,512]{1,0:T(8,128)(2,1)S(1)} %copy-done, ...), custom_call_target="tpu_custom_call" | custom-call | tf_op jit(solution)/shard_map/pallas_call | solution.py:239
  59.0 0.0 copy-start.1
  59.0 50.7 %all_to_all.11 = bf16[64,128,128]{2,1,0:T(8,128)(2,1)S(1)} all-to-all(bf16[64,128,128]{2,1,0:T(8,128)(2,1)S(1)} %bitcast.7), channel_id=1, replica_groups=mesh['row'=4,'col'=16,'tm'=4] {'col','tm'}, dimensions={0} | all-to-all | bytes 4194304 | tf_op jit(solution)/shard_map/all_to_all | solution.py:245
  109.7 0.0 copy-done.1
  109.7 1.9 %shard_map.67 = bf16[8,256,256]{2,1,0:T(8,128)(2,1)} custom-call(bf16[8192,128]{1,0:T(8,128)(2,1)S(1)} %bitcast.6, bf16[512,256]{1,0:T(8,128)(2,1)S(1)} %copy-done.1), custom_call_target="tpu_custom_call" | custom-call | tf_op jit(solution)/shard_map/pallas_call | solution.py:247
  (1 shorter events, 0.0 us)
Async XLA Ops:
  3.8 44.7 %copy-start = (bf16[512,512]{1,0:T(8,128)(2,1)S(1)}, bf16[512,512]{1,0:T(8,128)(2,1)}, u32[]{:S(2)}) copy-start(bf16[512,512]{1,0:T(8,128)(2,1)} %constant.9.clone.swap_ref) | copy-start | bytes 1572868
  3.8 44.7 %copy-start.2 = (bf16[128,128]{1,0:T(8,128)(2,1)S(1)}, bf16[128,128]{1,0:T(8,128)(2,1)}, u32[]{:S(2)}) copy-start(bf16[128,128]{1,0:T(8,128)(2,1)} %constant.10.clone.flip_ref) | copy-start | bytes 98308
  44.1 13.7 %collective-permute-start = (bf16[8,4,4,16,128]{4,3,2,1,0:T(8,128)(2,1)S(1)}, bf16[8,4,4,16,128]{4,3,2,1,0:T(8,128)(2,1)S(1)}, u32[]{:S(2)}, u32[]{:S(2)}) collective-permute-start(bf16[8,4,4,16,128]{4,3,2,1,0:T(8,128)(2,1)S(1)} %bitcast.11), channel_id=1, source_target_pairs={{64,0},{128,64},{192,128},{65,1},{129,65},{193,129},{66,2},{130,66... | collective-permute-start | bytes 1572872 | tf_op jit(solution)/shard_map/ppermute | solution.py:227
  59.0 50.7 %copy-start.1 = (bf16[512,256]{1,0:T(8,128)(2,1)S(1)}, bf16[512,256]{1,0:T(8,128)(2,1)}, u32[]{:S(2)}) copy-start(bf16[512,256]{1,0:T(8,128)(2,1)} %constant.11.clone.table_ref) | copy-start | bytes 786436

commit v11 on v8

--- a/solution.py
+++ b/solution.py
@@ -148,7 +148,8 @@
             cross_block(own[index, block], window[index, start : start + LANES + OFFS], index, block, out_ref)
 
 
-def far_kernel(halo_ref, window_ref, own_ref, swap_ref, near_ref, out_ref, beyond):
+def far_kernel(far_ref, chip_ref, window_ref, own_ref, swap_ref, near_ref, out_ref, halo_ref, beyond):
+    halo_ref[...] = far_ref[...] + chip_ref[...]
     swap = swap_ref[...]
     for index in range(BINS):
         place_tiles(halo_ref, swap, index, beyond, 0)
@@ -215,7 +216,8 @@
     some_bins = some_bins.reshape(ROW // 32, 4, BINS, 16, LANES)
 
     first = some_bins[: OFFS // 32]
-    halo = lax.ppermute(first, "row", [(1, 0), (2, 1), (3, 2)])
+    far_halo = lax.ppermute(first, "row", [(2, 1)])
+    chip_halo = lax.ppermute(first, "row", [(1, 0), (3, 2)])
     swap, flip = jnp.asarray(swap_table()), jnp.asarray(flip_table())
     near, window, own = call(
         near_kernel,
@@ -230,9 +232,12 @@
     cross = call(
         far_kernel,
         (GROUP, BINS, 2, 16, LANES),
-        [pltpu.VMEM((BINS, OFFS, 2 * LANES), jnp.bfloat16)],
+        [
+            pltpu.VMEM((OFFS // 32, 4, BINS, 16, LANES), jnp.bfloat16),
+            pltpu.VMEM((BINS, OFFS, 2 * LANES), jnp.bfloat16),
+        ],
         32,
-    )(halo, window, own, swap, near)
+    )(far_halo, chip_halo, window, own, swap, near)
     all_bins = lax.all_to_all(cross.reshape(GROUP, BINS * 32, LANES), GROUP_AXES, 0, 0, tiled=True)
 
     return call(

time: 112 us -> 112 us (level)
  blocking collectives: 91 us -> 88.3 us
  waiting for transfers between devices: 7.69 us -> 9.02 us
  starting transfers between devices: 4.33 us -> 5.65 us
    all_to_all x1, blocking collectives: 50.7 us -> 48 us  [body(): lax.all_to_all(cross.reshape(GROUP, BINS * 32, LANES), GROUP_AXES, 0, 0,...]
    ppermute x1 -> x2, waiting for transfers between devices: 7.69 us -> 9.02 us  [the longest x1 9.02 us: body(): far_halo = lax.ppermute(first, 'row', [(2, 1)])]
    ppermute x1 -> x2, starting transfers between devices: 4.33 us -> 5.65 us  [the longest x1 4.35 us: body(): chip_halo = lax.ppermute(first, 'row', [(1, 0), (3, 2)])]
  transfers between devices with their start and end apart: 1 -> 2, of which waited for: 1 -> 1; matrix products, arithmetic and copies ran while one was open for 0% -> 0% of each run, Pallas kernels for 1% -> 1%
where the time goes in v11:
time: 112 us
  blocking collectives  88.3 us (79%)
  waiting for transfers between devices  9.02 us (8%)
  Pallas kernels  8.54 us (8%)
  starting transfers between devices  5.65 us (5%)
    all_to_all x1, blocking collectives, body(): lax.all_to_all(cross.reshape(GROUP, BINS * 32, LANES), GROUP_AXES, 0, 0,...  48 us
    all_to_all x1, blocking collectives, body(): lax.all_to_all(whitened.reshape(GROUP, BINS, 16, LANES), GROUP_AXES, 0, 0...  40.3 us
    ppermute x1, waiting for transfers between devices, body(): far_halo = lax.ppermute(first, 'row', [(2, 1)])  9.02 us
    ppermute x1, starting transfers between devices, body(): chip_halo = lax.ppermute(first, 'row', [(1, 0), (3, 2)])  4.35 us
    pallas_call x1, Pallas kernels, body(): call(whiten_kernel, (HALF * 16, LANES), [pltpu.VMEM((16, HALF, LANES), jn...  3.75 us
  transfers between devices with their start and end apart: 2, of which 1 were waited for; matrix products, arithmetic and copies ran while one was open for 0% of the time, Pallas kernels for 1%

profile of v11, /device:TPU:1, one launch (start us, length us, event | category | flops | bytes accessed | tf_op | source)
XLA Modules:
  0.0 111.6 jit_solution(2599463190113795319)
XLA Ops:
  0.0 3.8 %shard_map.64 = bf16[4096,128]{1,0:T(8,128)(2,1)} custom-call(s32[32]{0:T(128)} %flags_ref.1, bf16[4,8,32,512]{3,2,1,0:T(8,128)(2,1)} %bitcast.10, bf16[512,512]{1,0:T(8,128)(2,1)} %constant.8.clone.table_ref), custom_call_target="tpu_custom_call" | custom-call | tf_op jit(solution)/shard_map/pallas_call | solution.py:203
  3.8 0.0 copy-start
  3.8 0.0 copy-start.2
  3.8 40.3 %all_to_all.10 = bf16[64,4,16,128]{3,2,1,0:T(8,128)(2,1)S(1)} all-to-all(bf16[64,4,16,128]{3,2,1,0:T(8,128)(2,1)} %bitcast.9), channel_id=1, replica_groups=mesh['row'=4,'col'=16,'tm'=4] {'col','tm'}, dimensions={0} | all-to-all | bytes 2097152 | tf_op jit(solution)/shard_map/all_to_all | solution.py:215
  44.1 4.4 %collective-permute-start.1 = (bf16[8,4,4,16,128]{4,3,2,1,0:T(8,128)(2,1)S(1)}, bf16[8,4,4,16,128]{4,3,2,1,0:T(8,128)(2,1)S(1)}, u32[]{:S(2)}, u32[]{:S(2)}) collective-permute-start(bf16[8,4,4,16,128]{4,3,2,1,0:T(8,128)(2,1)S(1)} %bitcast.11), channel_id=1, source_target_pairs={{64,0},{192,128},{65,1},{193,129},{66,2},{194,130},{67,3},{195,131... | collective-permute-start | bytes 1572872 | tf_op jit(solution)/shard_map/ppermute | solution.py:220
  48.5 1.3 %collective-permute-start = (bf16[8,4,4,16,128]{4,3,2,1,0:T(8,128)(2,1)S(1)}, bf16[8,4,4,16,128]{4,3,2,1,0:T(8,128)(2,1)S(1)}, u32[]{:S(2)}, u32[]{:S(2)}) collective-permute-start(bf16[8,4,4,16,128]{4,3,2,1,0:T(8,128)(2,1)S(1)} %bitcast.12), channel_id=1, source_target_pairs={{128,64},{129,65},{130,66},{131,67},{132,68},{133,69},{134,70},{13... | collective-permute-start | bytes 1572872 | tf_op jit(solution)/shard_map/ppermute | solution.py:219
  49.8 0.0 copy-done
  49.8 0.0 copy-done.2
  49.8 1.6 %shard_map.65 = (bf16[32,4,2,16,128]{4,3,2,1,0:T(8,128)(2,1)S(1)}, bf16[4,512,256]{2,1,0:T(8,128)(2,1)S(1)}, bf16[4,4,256,256]{3,2,1,0:T(8,128)(2,1)S(1)}) custom-call(bf16[16,4,4,16,128]{4,3,2,1,0:T(8,128)(2,1)S(1)} %bitcast.8, bf16[512,512]{1,0:T(8,128)(2,1)S(1)} %copy-done, bf16[128,128]{1,0:T(8,128)(2,1)S(1)} %copy-done.2), custom_call_target="tpu_custom_call" | custom-call | tf_op jit(solution)/shard_map/pallas_call | solution.py:222
  51.4 0.0 collective-permute-done.1.chip_ref
  51.4 9.0 %collective-permute-done.far_ref = bf16[8,4,4,16,128]{4,3,2,1,0:T(8,128)(2,1)S(1)} collective-permute-done((bf16[8,4,4,16,128]{4,3,2,1,0:T(8,128)(2,1)S(1)}, bf16[8,4,4,16,128]{4,3,2,1,0:T(8,128)(2,1)S(1)}, u32[]{:S(2)}, u32[]{:S(2)}) %collective-permute-start) | collective-permute-done | bytes 524320 | tf_op jit(solution)/shard_map/ppermute | solution.py:219
  60.5 1.2 %shard_map.66 = bf16[64,4,2,16,128]{4,3,2,1,0:T(8,128)(2,1)S(1)} custom-call(bf16[8,4,4,16,128]{4,3,2,1,0:T(8,128)(2,1)S(1)} %collective-permute-done.far_ref, bf16[8,4,4,16,128]{4,3,2,1,0:T(8,128)(2,1)S(1)} %collective-permute-done.1.chip_ref, bf16[4,512,256]{2,1,0:T(8,128)(2,1)S(1)} %get-tuple-element.8.window_ref, ...), custom_call_target="tpu_custom_call" | custom-call | tf_op jit(solution)/shard_map/pallas_call | solution.py:232
  61.7 0.0 copy-start.1
  61.7 48.0 %all_to_all.11 = bf16[64,128,128]{2,1,0:T(8,128)(2,1)S(1)} all-to-all(bf16[64,128,128]{2,1,0:T(8,128)(2,1)S(1)} %bitcast.7), channel_id=1, replica_groups=mesh['row'=4,'col'=16,'tm'=4] {'col','tm'}, dimensions={0} | all-to-all | bytes 4194304 | tf_op jit(solution)/shard_map/all_to_all | solution.py:241
  109.7 0.0 copy-done.1
  109.7 1.9 %shard_map.67 = bf16[8,256,256]{2,1,0:T(8,128)(2,1)} custom-call(bf16[8192,128]{1,0:T(8,128)(2,1)S(1)} %bitcast.6, bf16[512,256]{1,0:T(8,128)(2,1)S(1)} %copy-done.1), custom_call_target="tpu_custom_call" | custom-call | tf_op jit(solution)/shard_map/pallas_call | solution.py:243
  (1 shorter events, 0.0 us)
Async XLA Ops:
  3.8 46.0 %copy-start = (bf16[512,512]{1,0:T(8,128)(2,1)S(1)}, bf16[512,512]{1,0:T(8,128)(2,1)}, u32[]{:S(2)}) copy-start(bf16[512,512]{1,0:T(8,128)(2,1)} %constant.9.clone.swap_ref) | copy-start | bytes 1572868
  3.8 46.0 %copy-start.2 = (bf16[128,128]{1,0:T(8,128)(2,1)S(1)}, bf16[128,128]{1,0:T(8,128)(2,1)}, u32[]{:S(2)}) copy-start(bf16[128,128]{1,0:T(8,128)(2,1)} %constant.10.clone.flip_ref) | copy-start | bytes 98308
  44.1 7.3 %collective-permute-start.1 = (bf16[8,4,4,16,128]{4,3,2,1,0:T(8,128)(2,1)S(1)}, bf16[8,4,4,16,128]{4,3,2,1,0:T(8,128)(2,1)S(1)}, u32[]{:S(2)}, u32[]{:S(2)}) collective-permute-start(bf16[8,4,4,16,128]{4,3,2,1,0:T(8,128)(2,1)S(1)} %bitcast.11), channel_id=1, source_target_pairs={{64,0},{192,128},{65,1},{193,129},{66,2},{194,130},{67,3},{195,131... | collective-permute-start | bytes 1572872 | tf_op jit(solution)/shard_map/ppermute | solution.py:220
  48.5 12.0 %collective-permute-start = (bf16[8,4,4,16,128]{4,3,2,1,0:T(8,128)(2,1)S(1)}, bf16[8,4,4,16,128]{4,3,2,1,0:T(8,128)(2,1)S(1)}, u32[]{:S(2)}, u32[]{:S(2)}) collective-permute-start(bf16[8,4,4,16,128]{4,3,2,1,0:T(8,128)(2,1)S(1)} %bitcast.12), channel_id=1, source_target_pairs={{128,64},{129,65},{130,66},{131,67},{132,68},{133,69},{134,70},{13... | collective-permute-start | bytes 1572872 | tf_op jit(solution)/shard_map/ppermute | solution.py:219
  61.7 48.0 %copy-start.1 = (bf16[512,256]{1,0:T(8,128)(2,1)S(1)}, bf16[512,256]{1,0:T(8,128)(2,1)}, u32[]{:S(2)}) copy-start(bf16[512,256]{1,0:T(8,128)(2,1)} %constant.11.clone.table_ref) | copy-start | bytes 786436
